TPU v7x, 512 devices: a whole 4x8x8 slice. The times are simulated.
512 devices in a mesh: grp: 8 (over z), seg: 64 (over x, y, core).
Axes of the slice: x: 4, y: 8, z: 8, core: 2. Of those that a mesh axis runs over, the one named last changes fastest.
Arguments:
- bricks: bfloat16 [28, 3072, 512], P(None, 'seg'), may hold values from -6 to 6
- requests: int32 [64, 8, 64, 2], P('seg', 'grp'), may hold values from 0 to 47
- seg_owner: int32 [64, 1024, 1], P('seg', 'grp'), may hold values from 0 to 63; in each aligned block of 128 rows (0 to 127, 128 to 255, ..., all dimensions but the last counted through in order) at most 4 rows name the same one
- seg_slot: int32 [64, 1024], P('seg', 'grp'), may hold values from 0 to 1
- sample_cells: int32 [16, 64, 1024], P(None, 'seg', 'grp'), may hold values from 0 to 342
- sample_fracs: float32 [3, 16, 64, 1024], P(None, None, 'seg', 'grp'), may hold values from 0 to 1
- ray_angles: float32 [2, 1024], P(None, 'grp'), may hold values from -3.140625 to 3.140625
- ray_step: float32 [1024], P('grp'), may hold values from 0.0003 to 0.003
- pixel_target: float32 [3, 1024], P(None, 'grp'), may hold values from 0 to 1
Outputs:
- gradients: float32 [28, 3072, 512], P(None, 'seg')
- colour: float32 [3, 1024], P(None, 'grp')
Inputs may be any that keep to these rules, and one draw needn't show every extreme that they name: `seg_owner`: among the rays of one device, at most 4 segments name the same owner, a bound that some block reaches of them. `requests`: indices may repeat.
All inputs are finite; a program needn't handle non-finite values.
Results may differ from a plain program's by a relative error of at most 0.0003.
Values may be sent and summed in bfloat16 or wider, within the bound.
A program may use at most 128 MiB of HBM per device.

v0:
```python
from functools import partial

import jax
import jax.numpy as jnp
from jax import lax
from jax.sharding import PartitionSpec as P

COEF = 28
VOXELS = 512
CAP = 2


loss_scale = 1024.0


def entering(part, axis, combine, identity, reverse):
    count = lax.axis_size(axis)
    place = lax.axis_index(axis)
    ahead = count - 1 - place if reverse else place
    gathered = lax.all_gather(part, axis)
    state = jnp.zeros_like(part) + jnp.asarray(identity, part.dtype)

    def one(turn, state):
        source = count - 1 - turn if reverse else turn
        return combine(state, lax.dynamic_index_in_dim(gathered, source, 0, False))

    return lax.fori_loop(0, ahead, one, state)


def harmonics(ray_angles):
    polar = ray_angles[0]
    azimuth = ray_angles[1]
    coord_x = jnp.sin(polar) * jnp.cos(azimuth)
    coord_y = jnp.sin(polar) * jnp.sin(azimuth)
    coord_z = jnp.cos(polar)
    return jnp.stack(
        [
            0.28209479 * jnp.ones_like(coord_x),
            -0.48860251 * coord_y,
            0.48860251 * coord_z,
            -0.48860251 * coord_x,
            1.09254843 * coord_x * coord_y,
            -1.09254843 * coord_y * coord_z,
            0.31539157 * (2.0 * coord_z * coord_z - coord_x * coord_x - coord_y * coord_y),
            -1.09254843 * coord_x * coord_z,
            0.54627422 * (coord_x * coord_x - coord_y * coord_y),
        ]
    )


def corners(brick_ids, cell_ids, fraction):
    cell_x = cell_ids // 49
    cell_y = cell_ids // 7 % 7
    cell_z = cell_ids % 7
    base = brick_ids[None, :] * 512 + cell_x * 64 + cell_y * 8 + cell_z
    corner_ids = []
    weights = []
    for corner in range(8):
        along_x = corner // 4
        along_y = corner // 2 % 2
        along_z = corner % 2
        corner_ids.append(base + (along_x * 64 + along_y * 8 + along_z))
        weight_x = fraction[0] if along_x else 1.0 - fraction[0]
        weight_y = fraction[1] if along_y else 1.0 - fraction[1]
        weight_z = fraction[2] if along_z else 1.0 - fraction[2]
        weights.append(weight_x * weight_y * weight_z)
    return (jnp.stack(corner_ids), jnp.stack(weights))


def shade(corner_vals, weights, basis_rows, step_len):
    coefficient = jnp.sum(corner_vals * weights[None], axis=1)
    optical = jax.nn.softplus(coefficient[0]) * step_len[None]
    shaped = coefficient[1:].reshape(3, 9, coefficient.shape[1], coefficient.shape[2])
    logits = jnp.sum(shaped * basis_rows[None, :, None, :], axis=1)
    radiance = jax.nn.sigmoid(logits)
    before = jnp.cumsum(optical, axis=0) - optical
    seg_colour = jnp.sum(
        jnp.exp(-before)[None] * (1.0 - jnp.exp(-optical))[None] * radiance, axis=1
    )
    depth_total = jnp.sum(optical, axis=0)
    return (seg_colour, depth_total)


def add_terms(earlier, later):
    return earlier + later


def local(
    bricks,
    requests,
    seg_owner,
    seg_slot,
    sample_cells,
    sample_fracs,
    ray_angles,
    ray_step,
    pixel_target,
):
    peer_count = lax.axis_size("seg")
    owned = bricks.shape[1]
    basis_rows = harmonics(ray_angles)
    owners = seg_owner[0, :, 0]
    chosen = seg_slot[0]
    wanted = requests[0, 0]
    cell_ids = sample_cells[:, 0]
    fraction = sample_fracs[:, :, 0]
    slot_code = owners * CAP + chosen
    asked_ids = lax.all_to_all(wanted, "seg", split_axis=0, concat_axis=0, tiled=True)
    outgoing = jnp.take(bricks, asked_ids.reshape(-1), axis=1).reshape(
        COEF, peer_count, CAP, VOXELS
    )
    brick_table = lax.all_to_all(outgoing, "seg", split_axis=1, concat_axis=1, tiled=True).reshape(
        COEF, peer_count * CAP * VOXELS
    )
    corner_ids, weights = corners(slot_code, cell_ids, fraction)
    corner_vals = brick_table[:, corner_ids].astype(jnp.float32)
    local_shade = partial(shade, weights=weights, basis_rows=basis_rows, step_len=ray_step)
    (seg_colour, seg_tau), pullback = jax.vjp(local_shade, corner_vals)
    prefix = entering(seg_tau, "seg", add_terms, jnp.zeros_like(seg_tau), False)
    attenuation = jnp.exp(-prefix)
    contrib = attenuation[None] * seg_colour
    colour = lax.psum(contrib, "seg")
    suffix = entering(contrib, "seg", add_terms, jnp.zeros_like(contrib), True)
    misfit = loss_scale * (colour - pixel_target)
    grad_colour = attenuation[None] * misfit
    grad_tau = -jnp.sum(misfit * suffix, axis=0)
    (grad_vals,) = pullback((grad_colour, grad_tau))
    grad_table = (
        jnp.zeros((COEF, peer_count * CAP * VOXELS), jnp.float32).at[:, corner_ids].add(grad_vals)
    )
    returned = lax.all_to_all(
        grad_table.reshape(COEF, peer_count, CAP, VOXELS),
        "seg",
        split_axis=1,
        concat_axis=1,
        tiled=True,
    )
    grad_local = (
        jnp.zeros((COEF, owned, VOXELS), jnp.float32)
        .at[:, asked_ids.reshape(-1)]
        .add(returned.reshape(COEF, peer_count * CAP, VOXELS))
    )
    gradients = lax.psum(grad_local, "grp")
    return (gradients, colour)


def solution(mesh):
    return jax.shard_map(
        local,
        mesh=mesh,
        in_specs=(
            P(None, "seg", None),
            P("seg", "grp", None, None),
            P("seg", "grp", None),
            P("seg", "grp"),
            P(None, "seg", "grp"),
            P(None, None, "seg", "grp"),
            P(None, "grp"),
            P("grp"),
            P(None, "grp"),
        ),
        out_specs=(P(None, "seg", None), P(None, "grp")),
        check_vma=False,
    )
```

profile of v0, /device:TPU:1, one launch (start us, length us, event | category | flops | bytes accessed | tf_op | source)
XLA Modules:
  0.0 914.8 jit_solution(15444889397579738714)
XLA Ops:
  7.2 0.0 copy-start
  7.2 0.9 copy.56
  8.1 20.7 %all_to_all.19 = s32[64,1,2]{2,1,0:T(1,128)S(1)} all-to-all(s32[64,1,2]{2,1,0:T(1,128)S(1)} %copy.56), channel_id=1, replica_groups=mesh['grp'=8,'seg'=64] {'seg'}, dimensions={0} | all-to-all | bytes 1024 | tf_op jit(solution)/shard_map/all_to_all | solution.py:108
  28.8 0.5 broadcast.3240
  29.3 0.7 reduce.5
  30.0 0.1 reshape.1876
  30.2 0.0 copy-done
  30.2 13.0 %gather_fusion = bf16[128,28,512]{2,0,1:T(8,128)(2,1)} fusion(bf16[28,48,512]{2,1,0:T(8,128)(2,1)S(1)} %copy-done, s32[1024]{0:T(1024)S(1)} %pad_clamp_fusion), kind=kCustom, calls=%fused_computation | custom fusion | bytes 7340544 | tf_op jit(solution)/shard_map/jit(_take)/gather | solution.py:109
  43.1 7.0 gather.10
  50.2 0.1 copy.62
  50.3 0.1 copy.63
  50.4 0.0 copy-start.6
  50.4 0.0 copy-start.3
  50.4 0.0 copy-start.8
  50.4 0.0 copy-start.9
  50.4 0.0 copy-start.2
  50.5 7.2 broadcast_select_fusion
  57.6 5.6 all-to-all-start.1
  63.3 0.0 all-reduce.4.cloned.1.call-start
  63.3 0.0 copy-done.6
  63.3 0.1 subtract_multiply_fusion.4
  63.5 0.0 copy-done.3
  63.5 0.7 div.281
  64.2 0.0 copy-done.8
  64.2 0.0 copy-done.9
  64.2 0.0 copy-done.2
  64.5 83.5 %all-to-all-done.1 = bf16[28,64,2,512]{3,2,0,1:T(2,128)(2,1)} async-done(((bf16[28,64,2,512]{3,2,0,1:T(2,128)(2,1)}), bf16[28,64,2,512]{3,2,0,1:T(2,128)(2,1)}, u32[]{:S(2)}, u32[]{:S(2)}) %all-to-all-start.1) | async-done | bytes 3670048 | tf_op jit(solution)/shard_map/all_to_all | solution.py:112
  148.0 17.8 %copy.65 = bf16[28,64,2,512]{0,3,2,1:T(8,128)(2,1)} copy(bf16[28,64,2,512]{3,2,0,1:T(2,128)(2,1)} %all-to-all-done.1) | data formatting | bytes 7340032 | tf_op jit(solution)/shard_map/all_to_all | solution.py:112
  165.8 0.0 copy-start.4
  165.8 0.0 copy-start.7
  165.8 62.9 %gather_fusion.1 = bf16[16384,28]{1,0:T(8,128)(2,1)} fusion(bf16[28,65536]{0,1:T(8,128)(2,1)} %bitcast.209, s32[16384]{0:T(1024)S(1)} %broadcast_clamp_fusion), kind=kCustom, calls=%fused_computation.1 | custom fusion | bytes 1900544 | tf_op jit(solution)/shard_map/gather | solution.py:116
  228.7 4.5 fusion.2
  233.2 0.4 copy.69
  233.6 0.0 copy-done.4
  233.8 33.9 %all-gather.1 = f32[64,1,128]{2,1,0:T(1,128)S(1)} all-gather(f32[1,1,128]{2,1,0:T(1,128)S(1)} %bitcast.235), channel_id=2, replica_groups=mesh['grp'=8,'seg'=64] {'seg'}, dimensions={0}, use_global_device_ids=true | all-gather | bytes 33280 | tf_op jit(solution)/shard_map/all_gather | solution.py:20
  267.8 123.8 %psum.14 = f32[3,128]{1,0:T(4,128)S(1)} all-reduce(f32[3,128]{1,0:T(4,128)S(1)} %broadcast_multiply_fusion.2), channel_id=1, replica_groups=mesh['grp'=8,'seg'=64] {'seg'}, use_global_device_ids=true, to_apply=%region_7.8 | all-reduce | flops 384 | bytes 3072 | tf_op jit(solution)/shard_map/psum | solution.py:122
  391.6 0.0 copy-start.5
  391.6 51.9 %all_gather.12 = f32[64,3,128]{2,1,0:T(4,128)S(1)} all-gather(f32[1,3,128]{2,1,0:T(4,128)S(1)} %bitcast_multiply_fusion.3), channel_id=1, replica_groups=mesh['grp'=8,'seg'=64] {'seg'}, dimensions={0}, use_global_device_ids=true | all-gather | bytes 99840 | tf_op jit(solution)/shard_map/all_gather | solution.py:20
  443.5 2.6 while.23
  446.1 0.0 copy-done.7
  446.4 0.4 copy.70
  446.7 4.6 broadcast_multiply_fusion
  451.4 100.8 %scatter_custom_fusion = f32[28,65536]{0,1:T(8,128)} fusion(s32[16384]{0:T(1024)S(1)} %bitcast.230, f32[16384,28]{1,0:T(8,128)} %bitcast.212, f32[]{:T(128)} %constant.72.clone.1), kind=kCustom, calls=%fused_computation.6 | custom fusion | flops 458752 | bytes 7340544 | tf_op jit(solution)/shard_map/scatter-add | solution.py:129
  552.2 0.0 copy-done.5
  552.2 24.2 %copy.71 = f32[28,64,2,512]{3,2,0,1:T(2,128)} copy(f32[28,64,2,512]{0,3,2,1:T(8,128)} %bitcast.208) | data formatting | bytes 14680064 | tf_op jit(solution)/shard_map/reshape | solution.py:132
  576.4 168.8 %all_to_all.20 = f32[28,64,2,512]{3,2,0,1:T(2,128)} all-to-all(f32[28,64,2,512]{3,2,0,1:T(2,128)} %copy.71), channel_id=1, replica_groups=mesh['grp'=8,'seg'=64] {'seg'}, dimensions={1} | all-to-all | bytes 14680064 | tf_op jit(solution)/shard_map/all_to_all | solution.py:131
  745.2 10.2 %copy.72 = f32[28,64,2,512]{3,2,1,0:T(2,128)} copy(f32[28,64,2,512]{3,2,0,1:T(2,128)} %all_to_all.20) | data formatting | bytes 14680064 | tf_op jit(solution)/shard_map/all_to_all | solution.py:131
  755.4 10.0 %reshape.1907 = f32[28,128,512]{2,1,0:T(8,128)} reshape(f32[28,64,2,512]{3,2,1,0:T(2,128)} %copy.72) | data formatting | bytes 14680064 | tf_op jit(solution)/shard_map/reshape | solution.py:141
  765.4 10.6 %copy.73 = f32[128,28,512]{2,1,0:T(8,128)} copy(f32[128,28,512]{2,0,1:T(8,128)} %bitcast.210) | data formatting | bytes 14680064 | tf_op jit(solution)/shard_map/reshape | solution.py:141
  776.0 2.2 broadcast_in_dim.48
  778.1 0.0 copy-start.1
  778.1 26.4 %scatter_fusion = f32[28,48,512]{2,0,1:T(8,128)} fusion(f32[28,48,512]{2,0,1:T(8,128)} %broadcast_in_dim.48, s32[128]{0:T(128)S(1)} %fusion.37, f32[128,28,512]{2,1,0:T(8,128)} %copy.73), kind=kCustom, calls=%fused_computation.3 | custom fusion | flops 1835008 | bytes 22020608 | tf_op jit(solution)/shard_map/scatter-add | solution.py:141
  804.6 0.0 all-reduce.4.cloned.1.call-update
  804.6 98.1 %all-reduce.4.cloned.1.call-done = f32[28,48,512]{2,0,1:T(8,128)} async-done(((f32[28,48,512]{2,0,1:T(8,128)}), f32[28,48,512]{2,0,1:T(8,128)}) %all-reduce.4.cloned.1.call-update) | async-done | bytes 2752528 | tf_op jit(solution)/shard_map/psum | solution.py:143
  902.7 5.0 copy.74
  907.7 0.0 copy-done.1
  (112 shorter events, 1.6 us)
Async XLA Ops:
  7.2 23.0 %copy-start = (bf16[28,48,512]{2,1,0:T(8,128)(2,1)S(1)}, bf16[28,48,512]{2,1,0:T(8,128)(2,1)}, u32[]{:S(2)}) copy-start(bf16[28,48,512]{2,1,0:T(8,128)(2,1)} %param.13) | copy-start | bytes 4128772
  50.4 12.9 %copy-start.6 = (f32[2,128]{1,0:T(2,128)S(1)}, f32[2,128]{1,0:T(2,128)}, u32[]{:S(2)}) copy-start(f32[2,128]{1,0:T(2,128)} %param.19) | copy-start | bytes 3076
  50.4 13.1 %copy-start.3 = (s32[16,1,128]{2,1,0:T(1,128)S(1)}, s32[16,1,128]{2,1,0:T(1,128)}, u32[]{:S(2)}) copy-start(s32[16,1,128]{2,1,0:T(1,128)} %param.17) | copy-start | bytes 24580
  50.4 13.8 %copy-start.8 = (s32[1,128]{1,0:T(1,128)S(1)}, s32[1,128]{1,0:T(1,128)}, u32[]{:S(2)}) copy-start(s32[1,128]{1,0:T(1,128)} %param.16) | copy-start | bytes 1540
  50.4 13.8 %copy-start.9 = (s32[1,128,1]{1,2,0:T(1,128)S(1)}, s32[1,128,1]{1,2,0:T(1,128)}, u32[]{:S(2)}) copy-start(s32[1,128,1]{1,2,0:T(1,128)} %param.15) | copy-start | bytes 1540
  50.4 13.8 %copy-start.2 = (f32[3,16,1,128]{3,2,1,0:T(1,128)S(1)}, f32[3,16,1,128]{3,2,1,0:T(1,128)}, u32[]{:S(2)}) copy-start(f32[3,16,1,128]{3,2,1,0:T(1,128)} %param.18) | copy-start | bytes 73732
  57.6 90.4 %all-to-all-start.1 = ((bf16[28,64,2,512]{3,2,0,1:T(2,128)(2,1)}), bf16[28,64,2,512]{3,2,0,1:T(2,128)(2,1)}, u32[]{:S(2)}, u32[]{:S(2)}) async-start(bf16[28,64,2,512]{3,2,0,1:T(2,128)(2,1)} %broadcast_select_fusion), calls=%async_computation.1 | async-start | bytes 7340032 | tf_op jit(solution)/shard_map/all_to_all | solution.py:112
  63.3 839.4 %all-reduce.4.cloned.1.call-start = ((), (), s32[]{:S(2)}) async-start(), calls=%async_computation.3 | async-start | bytes 6291456 | tf_op jit(solution)/shard_map/psum | solution.py:143
  165.8 67.8 %copy-start.4 = (f32[128]{0:T(128)S(1)}, f32[128]{0:T(128)}, u32[]{:S(2)}) copy-start(f32[128]{0:T(128)} %param.20) | copy-start | bytes 1540
  165.8 280.3 %copy-start.7 = (f32[3,128]{1,0:T(4,128)S(1)}, f32[3,128]{1,0:T(4,128)}, u32[]{:S(2)}) copy-start(f32[3,128]{1,0:T(4,128)} %param.21) | copy-start | bytes 4612
  391.6 160.6 %copy-start.5 = (f32[3,128]{1,0:T(4,128)}, f32[3,128]{1,0:T(4,128)S(1)}, u32[]{:S(2)}) copy-start(f32[3,128]{1,0:T(4,128)S(1)} %psum.14) | copy-start | bytes 4612
  778.1 129.5 %copy-start.1 = (bf16[28,48,512]{2,1,0:T(8,128)(2,1)S(1)}, bf16[28,48,512]{2,1,0:T(8,128)(2,1)}, u32[]{:S(2)}) copy-start(bf16[28,48,512]{2,1,0:T(8,128)(2,1)} %param.13) | copy-start | bytes 4128772
Sparse Core Ops, SparseCore 0:
  804.7 97.9 all-reduce.3
where the time goes:
time: 926 us; the launch traced here: 915 us
  blocking collectives  399 us (43%)
  waiting for transfers between devices  182 us (20%)
  local copies, waits for them, and re-layouts  165 us (18%)
  other arithmetic  146 us (16%)
  between operations  14.7 us (2%)
    all_to_all x1, blocking collectives, local(): lax.all_to_all(grad_table.reshape(COEF, peer_count, CAP, VOXELS), 'seg',...  169 us
    psum x1, blocking collectives, local(): colour = lax.psum(contrib, 'seg')  124 us
    scatter-add x1, other arithmetic, local(): jnp.zeros((COEF, peer_count * CAP * VOXELS), jnp.float32).at[:, corner_ids]  101 us
    psum x1, waiting for transfers between devices, local(): gradients = lax.psum(grad_local, 'grp')  98.1 us
    all_gather x2, blocking collectives, entering(): gathered = lax.all_gather(part, axis)  85.9 us
    all_to_all x1, waiting for transfers between devices, local(): lax.all_to_all(outgoing, 'seg', split_axis=1, concat_axis=1, tiled=True)  83.5 us
    gather x1, local copies, waits for them, and re-layouts, local(): corner_vals = brick_table[:, corner_ids].astype(jnp.float32)  62.9 us
    scatter-add x1, other arithmetic, local(): grad_local = jnp.zeros((COEF, owned, VOXELS), jnp.float32).at[:, asked_id...  26.4 us
  transfers between devices with their start and end apart: 2, of which 2 were waited for; matrix products, arithmetic and copies ran while one was open for 0% of the time, Pallas kernels for 0%

commit v1 on v0

v1 whole, which is shorter than its diff:
```python
import functools

import jax
import jax.numpy as jnp
from jax import lax
from jax.experimental import pallas as pl
from jax.experimental.pallas import tpu as pltpu
from jax.sharding import PartitionSpec as P

COEF = 28
VOXELS = 512
SAMP = 16
OWNERS = 64
GROUPS = 8
SLOTS = 4
BRICKS = 48
RAYS = 128
CHUNKS = OWNERS * SLOTS // 8
ALL_CHUNKS = GROUPS * CHUNKS
TABLE = 384
UNROLL = 4
LOSS_SCALE = 1024.0
F32 = jnp.float32
BF16 = jnp.bfloat16
I32 = jnp.int32
VMEM = pl.BlockSpec(memory_space=pltpu.VMEM)
ANY = pl.BlockSpec(memory_space=pl.ANY)
MESH = pl.DeviceIdType.MESH
NN = (((1,), (0,)), ((), ()))
NT = (((1,), (1,)), ((), ()))


def iota(shape, dim):
    return lax.broadcasted_iota(I32, shape, dim)


def exact_dot(a, b, dims=NN):
    return lax.dot_general(
        a, b, dims, precision=lax.Precision.HIGHEST, preferred_element_type=F32
    )


def fast_dot(a, b, dims=NN):
    return lax.dot_general(a, b, dims, preferred_element_type=F32)


def split(value):
    high = value.astype(BF16)
    return high, (value - high.astype(F32)).astype(BF16)


def hat(place):
    return jnp.maximum(1.0 - jnp.abs(place - iota((8, 128), 0).astype(F32)), 0.0)


def softplus(value):
    return jnp.maximum(value, 0.0) + jnp.log1p(jnp.exp(-jnp.abs(value)))


def sigmoid(value):
    return 1.0 / (1.0 + jnp.exp(-value))


def ray_basis(angles):
    polar = angles[0:1]
    azimuth = angles[1:2]
    x = jnp.sin(polar) * jnp.cos(azimuth)
    y = jnp.sin(polar) * jnp.sin(azimuth)
    z = jnp.cos(polar)
    return [
        0.28209479 * jnp.ones_like(x),
        -0.48860251 * y,
        0.48860251 * z,
        -0.48860251 * x,
        1.09254843 * x * y,
        -1.09254843 * y * z,
        0.31539157 * (2.0 * z * z - x * x - y * y),
        -1.09254843 * x * z,
        0.54627422 * (x * x - y * y),
    ]


def pack(owner, slot, wanted, cells, fracs, basis, step):
    mine = owner == iota((OWNERS, RAYS), 0)
    ones = jnp.where(mine, 1.0, 0.0)
    upper = jnp.where(iota((RAYS, RAYS), 0) < iota((RAYS, RAYS), 1), 1.0, 0.0)
    earlier = fast_dot(ones.astype(BF16), upper.astype(BF16))
    rank = jnp.sum(ones * earlier, axis=0, keepdims=True)
    named = wanted.astype(F32)
    brick = jnp.sum(
        ones * jnp.where(slot == 0, named[:, 0:1], named[:, 1:2]), axis=0, keepdims=True
    )
    choice = jnp.concatenate(
        [jnp.where(rank == float(j), ones, 0.0) for j in range(SLOTS)], axis=1
    )
    cell_x = (cells * 1338) >> 16
    rest = cells - cell_x * 49
    cell_y = (rest * 9363) >> 16
    cell_z = rest - cell_y * 7
    place_x = cell_x.astype(F32) + fracs[0:16]
    place_y = cell_y.astype(F32) + fracs[16:32]
    place_z = cell_z.astype(F32) + fracs[32:48]
    row = iota((SAMP, RAYS), 0)
    extra = jnp.where(row == 11, 1.0, 0.0)
    for k, value in enumerate(basis + [step, brick + 1.0]):
        extra = jnp.where(row == k, value, extra)
    none = jnp.zeros((SAMP, RAYS), F32)

    def placed(first, second):
        parts = []
        for j in range(SLOTS):
            rows = [none] * 8
            rows[j] = first
            rows[4 + j] = second
            parts.append(jnp.concatenate(rows, axis=0))
        return jnp.concatenate(parts, axis=1)

    return (
        choice,
        exact_dot(choice, placed(place_x, place_y), NT),
        exact_dot(choice, placed(place_z, extra), NT),
    )


def greet(axes):
    barrier = pltpu.get_barrier_semaphore()
    total = 0
    for axis, count in axes:
        me = lax.axis_index(axis)

        def hail(turn, carry, axis=axis, count=count, me=me):
            pl.semaphore_signal(
                barrier,
                inc=1,
                device_id={axis: lax.rem(me + turn, count)},
                device_id_type=MESH,
            )
            return carry

        lax.fori_loop(1, count, hail, 0)
        total += count - 1
    pl.semaphore_wait(barrier, total)


def send_all(axis, count, source, target, send_sem, recv_sem):
    me = lax.axis_index(axis)

    def one(turn, carry):
        peer = lax.rem(me + turn, count)
        pltpu.make_async_remote_copy(
            src_ref=source(peer),
            dst_ref=target.at[me],
            send_sem=send_sem,
            recv_sem=recv_sem,
            device_id={axis: peer},
            device_id_type=MESH,
        ).start()
        return carry

    lax.fori_loop(1, count, one, 0)


def wait_all(target, count, sem):
    part = target.at[pl.ds(0, count - 1)]
    pltpu.make_async_copy(part, part, sem).wait()


def dispatch_kernel(
    owner_ref, slot_ref, wanted_ref, cells_ref, fracs_ref, angles_ref, step_ref,
    got_ref, choice_ref, out_ref, send_sem, recv_sem,
):
    greet([("seg", OWNERS)])
    choice, first, second = pack(
        owner_ref[...], slot_ref[...], wanted_ref[...], cells_ref[...], fracs_ref[...],
        ray_basis(angles_ref[...]), step_ref[...],
    )
    choice_ref[...] = choice
    out_ref[:, 0, :] = first
    out_ref[:, 1, :] = second
    me = lax.axis_index("seg")
    send_all("seg", OWNERS, lambda peer: out_ref.at[peer], got_ref, send_sem, recv_sem)
    got_ref[me] = out_ref[me]
    wait_all(got_ref, OWNERS, recv_sem)
    wait_all(out_ref, OWNERS, send_sem)


def dispatch(owner, slot, wanted, cells, fracs, angles, step):
    return pl.pallas_call(
        dispatch_kernel,
        out_shape=(
            jax.ShapeDtypeStruct((OWNERS, 2, 128), F32),
            jax.ShapeDtypeStruct((OWNERS, SLOTS * RAYS), F32),
        ),
        in_specs=[VMEM] * 7,
        out_specs=(VMEM, VMEM),
        scratch_shapes=[
            pltpu.VMEM((OWNERS, 2, 128), F32),
            pltpu.SemaphoreType.DMA,
            pltpu.SemaphoreType.DMA,
        ],
        compiler_params=pltpu.CompilerParams(
            collective_id=0, has_side_effects=True, vmem_limit_bytes=32 << 20
        ),
        name="dispatch",
    )(owner, slot, wanted, cells, fracs, angles, step)


def lane_group_sum():
    return jnp.where(iota((128, 128), 0) // 16 == iota((128, 128), 1) // 16, 1.0, 0.0)


def basis_rows(extra_row, group_sum):
    c = iota((32, 128), 0)
    k = lax.rem(c - 1 + 9, 9)
    wanted = jnp.where(c == 0, 11, jnp.where(c < COEF, k, 15))
    chosen = jnp.where(iota((32, 128), 1) % 16 == wanted, extra_row, 0.0)
    high, low = split(chosen)
    both = fast_dot(jnp.concatenate([high, low], axis=0), group_sum)
    return both[0:32] + both[32:64]


def forward_kernel(
    bricks_ref, got_ref, tiles_ref, sums_ref,
    wide_ref, brick_ref, half_ref, id_vmem, id_smem, place_ref, raw_ref, sem,
):
    wide_ref[...] = jnp.zeros_like(wide_ref)
    for c in range(COEF):
        for x in range(4):
            wide_ref[x, pl.ds(c, BRICKS, stride=32), :] = bricks_ref[
                c, :, x * 128 : x * 128 + 128
            ].astype(F32)

    def narrow(b, carry):
        rows = pl.ds(pl.multiple_of(b * 32, 32), 32)
        for x in range(4):
            brick_ref[rows, x * 128 : x * 128 + 128] = wide_ref[x, rows, :].astype(BF16)
        return carry

    lax.fori_loop(0, BRICKS, narrow, 0)

    left = iota((CHUNKS, 128), 1) < 64
    for half in range(2):
        half_ref[...] = got_ref[:, half, :]
        even = half_ref[pl.ds(0, CHUNKS, stride=2), :]
        odd = half_ref[pl.ds(1, CHUNKS, stride=2), :]
        place_ref[2 * half] = jnp.where(left, even, pltpu.roll(odd, 64, 1))
        place_ref[2 * half + 1] = jnp.where(left, pltpu.roll(even, 64, 1), odd)
    extra = place_ref[3]
    id_vmem[...] = jnp.maximum(extra - 1.0, 0.0).astype(I32)
    copy = pltpu.make_async_copy(id_vmem, id_smem, sem)
    copy.start()
    copy.wait()
    group_sum = lane_group_sum().astype(BF16)
    lane_group = iota((32, 128), 1) // 16
    c32 = iota((32, 128), 0)

    def one(chunk):
        hat_x = hat(place_ref[0, pl.ds(chunk, 1), :])
        hat_y = hat(place_ref[1, pl.ds(chunk, 1), :])
        hat_z = hat(place_ref[2, pl.ds(chunk, 1), :])
        plane = jnp.concatenate([hat_y[y : y + 1] * hat_z for y in range(8)], axis=0)
        weights = jnp.concatenate([hat_x[x : x + 1] * plane for x in range(8)], axis=0)
        high, low = split(weights)
        rows = []
        for seg in range(8):
            b = id_smem[chunk, seg * 16 + 10]
            rows.append(brick_ref[pl.ds(pl.multiple_of(b * 32, 32), 32), :])
        values = fast_dot(
            jnp.concatenate(rows, axis=0), jnp.concatenate([high, low], axis=1)
        )
        coef = jnp.zeros((32, 128), F32)
        for seg in range(8):
            part = values[seg * 32 : seg * 32 + 32]
            coef = jnp.where(lane_group == seg, part[:, 0:128] + part[:, 128:256], coef)
        shaped = coef * basis_rows(place_ref[3, pl.ds(chunk, 1), :], group_sum)
        raw_ref[0, pl.ds(chunk, 1), :] = coef[0:1]
        for ch in range(3):
            inside = (c32 >= 1 + 9 * ch) & (c32 < 10 + 9 * ch)
            raw_ref[1 + ch, pl.ds(chunk, 1), :] = jnp.sum(
                jnp.where(inside, shaped, 0.0), axis=0, keepdims=True
            )

    def several(turn, carry):
        for k in range(2):
            one(turn * 2 + k)
        return carry

    lax.fori_loop(0, CHUNKS // 2, several, 0)

    for q in range(3):
        tiles_ref[pl.ds(q, CHUNKS, stride=8), :] = place_ref[q]
    for q in range(4):
        tiles_ref[pl.ds(3 + q, CHUNKS, stride=8), :] = raw_ref[q]
    tiles_ref[pl.ds(7, CHUNKS, stride=8), :] = extra

    optical, through, opaque, _ = march(raw_ref[0], extra)
    light = through * opaque
    total = jnp.zeros((CHUNKS, 128), F32)
    row, lane = iota((128, 128), 0), iota((128, 128), 1)
    for v in range(4):
        part = optical if v == 3 else light * sigmoid(raw_ref[1 + v])
        total += exact_dot(part, jnp.where(lane == (row // 16) * 8 + v, 1.0, 0.0))
    sums_ref[:, 0, :] = total


def march(density, extra):
    row, lane = iota((128, 128), 0), iota((128, 128), 1)
    same = row // 16 == lane // 16
    step = exact_dot(extra, jnp.where(same & (row % 16 == 9), 1.0, 0.0))
    optical = softplus(density) * step
    before = exact_dot(optical, jnp.where(same & (row < lane), 1.0, 0.0))
    through = jnp.exp(-before)
    remains = jnp.exp(-optical)
    return optical, through, 1.0 - remains, (step, remains)


def forward(bricks, got):
    return pl.pallas_call(
        forward_kernel,
        out_shape=(
            jax.ShapeDtypeStruct((CHUNKS * 8, 128), F32),
            jax.ShapeDtypeStruct((CHUNKS, 1, 128), F32),
        ),
        in_specs=[VMEM, VMEM],
        out_specs=(VMEM, VMEM),
        scratch_shapes=[
            pltpu.VMEM((4, BRICKS * 32, 128), F32),
            pltpu.VMEM((BRICKS * 32, VOXELS), BF16),
            pltpu.VMEM((OWNERS, 128), F32),
            pltpu.VMEM((CHUNKS, 128), I32),
            pltpu.SMEM((CHUNKS, 128), I32),
            pltpu.VMEM((4, CHUNKS, 128), F32),
            pltpu.VMEM((4, CHUNKS, 128), F32),
            pltpu.SemaphoreType.DMA,
        ],
        compiler_params=pltpu.CompilerParams(vmem_limit_bytes=40 << 20),
        name="interpolate",
    )(bricks, got)


def to_rays(sums, choice):
    half = lax.rem(lax.axis_index("seg"), 2)
    turned = pltpu.roll(sums, lax.rem(128 - half * 32, 128), 1)
    found = exact_dot(jnp.transpose(turned)[0:32], choice)
    total = jnp.zeros((8, RAYS), F32)
    for j in range(SLOTS):
        total += found[8 * j : 8 * j + 8, RAYS * j : RAYS * j + RAYS]
    return total


def composite(colours, taus, target):
    me = lax.axis_index("seg")
    lower = jnp.where(iota((OWNERS, OWNERS), 1) < iota((OWNERS, OWNERS), 0), 1.0, 0.0)
    through = jnp.exp(-exact_dot(lower, taus))
    depth = iota((OWNERS, RAYS), 0)
    here = jnp.sum(jnp.where(depth == me, through, 0.0), axis=0, keepdims=True)
    colour, grad_colour = [], []
    grad_tau = jnp.zeros((1, RAYS), F32)
    for v in range(3):
        contrib = through * colours[v]
        colour.append(jnp.sum(contrib, axis=0, keepdims=True))
        behind = jnp.sum(jnp.where(depth > me, contrib, 0.0), axis=0, keepdims=True)
        misfit = LOSS_SCALE * (colour[v] - target[v : v + 1])
        grad_colour.append(here * misfit)
        grad_tau -= misfit * behind
    return colour, grad_colour + [grad_tau]


def to_slots(grads, choice):
    me = lax.axis_index("seg")
    row = iota((SLOTS * 4, RAYS), 0)
    block = jnp.zeros((SLOTS * 4, RAYS), F32)
    for v in range(4):
        block = jnp.where(row % 4 == v, grads[v], block)
    wide = jnp.concatenate(
        [jnp.where(row // 4 == j, block, 0.0) for j in range(SLOTS)], axis=1
    )
    wide = jnp.concatenate([wide, jnp.zeros((112, SLOTS * RAYS), F32)], axis=0)
    placed = exact_dot(choice, wide, NT)
    return pltpu.roll(placed, (me // 16) * 32 + lax.rem(me, 2) * 16, 1)


def composite_kernel(
    sums_ref, tiles_ref, choice_ref, target_ref,
    colour_ref, all_tiles_ref, all_grads_ref,
    back_ref, ray_ref, rays_ref, slot_ref, slots_ref, grads_ref,
    send_sems, recv_sems, own_sem,
):
    greet([("seg", OWNERS), ("grp", GROUPS)])
    me = lax.axis_index("seg")
    group = lax.axis_index("grp")
    send_all(
        "grp", GROUPS, lambda peer: tiles_ref, all_tiles_ref, send_sems.at[0], recv_sems.at[0]
    )
    own = pltpu.make_async_copy(tiles_ref, all_tiles_ref.at[group], own_sem)
    own.start()

    send_all(
        "seg", OWNERS, lambda peer: sums_ref.at[peer // 2], back_ref,
        send_sems.at[1], recv_sems.at[1],
    )
    back_ref[me] = sums_ref[me // 2]
    wait_all(back_ref, OWNERS, recv_sems.at[1])
    choice = choice_ref[...]
    ray_ref[...] = to_rays(back_ref[:, 0, :], choice)[0:4]

    send_all("seg", OWNERS, lambda peer: ray_ref, rays_ref, send_sems.at[2], recv_sems.at[2])
    rays_ref[me] = ray_ref[...]
    wait_all(rays_ref, OWNERS, recv_sems.at[2])
    colour, grads = composite(
        [rays_ref[:, v, :] for v in range(3)], rays_ref[:, 3, :], target_ref[...]
    )
    for v in range(3):
        colour_ref[v : v + 1, :] = colour[v]
    slot_ref[:, 0, :] = to_slots(grads, choice)

    send_all(
        "seg", OWNERS, lambda peer: slot_ref.at[peer], slots_ref, send_sems.at[3], recv_sems.at[3]
    )
    slots_ref[me] = slot_ref[me]
    wait_all(slots_ref, OWNERS, recv_sems.at[3])
    pick = jnp.where((iota((8, OWNERS), 1) // 2) % 8 == iota((8, OWNERS), 0), 1.0, 0.0)
    grads_ref[...] = exact_dot(pick, slots_ref[:, 0, :])

    send_all(
        "grp", GROUPS, lambda peer: grads_ref, all_grads_ref, send_sems.at[4], recv_sems.at[4]
    )
    all_grads_ref[group] = grads_ref[...]
    wait_all(all_grads_ref, GROUPS, recv_sems.at[4])
    own.wait()
    wait_all(all_tiles_ref, GROUPS, recv_sems.at[0])
    wait_all(all_tiles_ref, GROUPS, send_sems.at[0])
    wait_all(back_ref, OWNERS, send_sems.at[1])
    wait_all(rays_ref, OWNERS, send_sems.at[2])
    wait_all(slots_ref, OWNERS, send_sems.at[3])
    wait_all(all_grads_ref, GROUPS, send_sems.at[4])


def exchange(sums, tiles, choice, target):
    return pl.pallas_call(
        composite_kernel,
        out_shape=(
            jax.ShapeDtypeStruct((3, RAYS), F32),
            jax.ShapeDtypeStruct((GROUPS, CHUNKS * 8, 128), F32),
            jax.ShapeDtypeStruct((GROUPS, 8, 128), F32),
        ),
        in_specs=[VMEM] * 4,
        out_specs=(VMEM, VMEM, VMEM),
        scratch_shapes=[
            pltpu.VMEM((OWNERS, 1, 128), F32),
            pltpu.VMEM((4, RAYS), F32),
            pltpu.VMEM((OWNERS, 4, RAYS), F32),
            pltpu.VMEM((OWNERS, 1, 128), F32),
            pltpu.VMEM((OWNERS, 1, 128), F32),
            pltpu.VMEM((8, 128), F32),
            pltpu.SemaphoreType.DMA((5,)),
            pltpu.SemaphoreType.DMA((5,)),
            pltpu.SemaphoreType.DMA,
        ],
        compiler_params=pltpu.CompilerParams(
            collective_id=1, has_side_effects=True, vmem_limit_bytes=32 << 20
        ),
        name="composite",
    )(sums, tiles, choice, target)


def plan_chunks(extra):
    across = jnp.transpose(extra)
    named = iota((64, ALL_CHUNKS), 0).astype(F32) + 1.0
    hits = [
        jnp.where(across[seg * 16 + 10 : seg * 16 + 11] == named, 1.0, 0.0) for seg in range(8)
    ]
    earlier = jnp.where(
        iota((ALL_CHUNKS, ALL_CHUNKS), 0) < iota((ALL_CHUNKS, ALL_CHUNKS), 1), 1.0, 0.0
    ).astype(BF16)
    counts = fast_dot(jnp.concatenate(hits, axis=0).astype(BF16), earlier)
    carry = jnp.zeros((64, 1), F32)
    ranks = []
    for seg in range(8):
        ranks.append(counts[seg * 64 : seg * 64 + 64] + carry)
        carry = carry + jnp.sum(hits[seg], axis=1, keepdims=True)
    full = jnp.floor((carry + 7.0) * 0.125)
    lower = jnp.where(iota((64, 64), 1) < iota((64, 64), 0), 1.0, 0.0).astype(BF16)
    full_wide = jnp.broadcast_to(full, (64, 128))
    start = fast_dot(lower, full_wide.astype(BF16))
    end = start + full_wide
    start256 = jnp.concatenate([start, start], axis=1)
    selectors, values = [], []
    row = iota((32, ALL_CHUNKS), 0)
    lane = iota((32, ALL_CHUNKS), 1).astype(F32)
    for seg in range(8):
        place = (
            jnp.sum(hits[seg] * (8.0 * start256 + ranks[seg] + 1.0), axis=0, keepdims=True) - 1.0
        )
        chunk = jnp.floor(place * 0.125)
        inside = place - 8.0 * chunk
        selectors.append(
            jnp.where(iota((TABLE, ALL_CHUNKS), 0).astype(F32) == chunk, 1.0, 0.0).astype(BF16)
        )
        kind = jnp.where(
            row < 8, lane, jnp.where(row < 16, float(seg), jnp.where(row < 24, 1.0, 0.0))
        )
        values.append(jnp.where((row % 8).astype(F32) == inside, kind, 0.0).astype(BF16))
    table = fast_dot(
        jnp.concatenate(values, axis=1), jnp.concatenate(selectors, axis=1), NT
    )
    tile = table[0:8] + (1.0 - table[16:24]) * float(ALL_CHUNKS)
    turn = 16.0 * (iota((8, TABLE), 0).astype(F32) - table[8:16])
    turn = jnp.where(turn < 0.0, turn + 128.0, turn)
    place = iota((64, 128), 1).astype(F32)
    real = iota((64, 128), 0) < BRICKS
    owner = [
        jnp.sum(jnp.where((end <= place + 128.0 * k) & real, 1.0, 0.0), axis=0, keepdims=True)
        for k in range(TABLE // 128)
    ]
    owner = jnp.minimum(jnp.concatenate(owner, axis=1), float(BRICKS - 1))
    number = jnp.sum(full_wide, axis=0, keepdims=True)
    number = jnp.concatenate([number] * (TABLE // 128), axis=1)
    last = jnp.where(iota((8, TABLE), 0) == 0, owner, number)
    return jnp.concatenate([tile, turn, last], axis=0).astype(I32)


def gradient_kernel(
    tiles_hbm, grads_ref, out_ref,
    tiles_ref, table_vmem, table_smem, slot_ref, total_ref, sems,
):
    load = pltpu.make_async_copy(tiles_hbm, tiles_ref.at[pl.ds(0, ALL_CHUNKS * 8)], sems.at[0])
    load.start()
    tiles_ref[pl.ds(ALL_CHUNKS * 8, 8), :] = jnp.zeros((8, 128), F32)
    row, lane = iota((128, 128), 0), iota((128, 128), 1)
    for part in range(4):
        for v in range(4):
            spread = jnp.where(row == part * 32 + (lane // 16) * 4 + v, 1.0, 0.0)
            wide = exact_dot(grads_ref[...], spread)
            for g in range(GROUPS):
                slot_ref[v, pl.ds(g * CHUNKS + part * 8, 8), :] = wide[g * 8 : g * 8 + 8]
    total_ref[...] = jnp.zeros_like(total_ref)
    load.wait()

    extra = tiles_ref[pl.ds(7, ALL_CHUNKS, stride=8), :]
    table_vmem[...] = plan_chunks(extra)
    plan = pltpu.make_async_copy(table_vmem, table_smem, sems.at[1])
    plan.start()

    density = tiles_ref[pl.ds(3, ALL_CHUNKS, stride=8), :]
    optical, through, opaque, (step, remains) = march(density, extra)
    light = through * opaque
    mixed = jnp.zeros((ALL_CHUNKS, 128), F32)
    for v in range(3):
        radiance = sigmoid(tiles_ref[pl.ds(4 + v, ALL_CHUNKS, stride=8), :])
        grad_colour = slot_ref[v]
        mixed += grad_colour * radiance
        tiles_ref[pl.ds(4 + v, ALL_CHUNKS, stride=8), :] = (
            grad_colour * light * radiance * (1.0 - radiance)
        )
    later = jnp.where((row // 16 == lane // 16) & (row > lane), 1.0, 0.0)
    grad_optical = through * remains * mixed - exact_dot(light * mixed, later) + slot_ref[3]
    tiles_ref[pl.ds(3, ALL_CHUNKS, stride=8), :] = grad_optical * step * sigmoid(density)
    plan.wait()

    group_sum = lane_group_sum().astype(BF16)
    lane_group = iota((8, 128), 1) // 16
    c32 = iota((32, 128), 0)

    def one(chunk):
        tile = jnp.zeros((8, 128), F32)
        for p in range(8):
            start = pl.multiple_of(table_smem[p, chunk] * 8, 8)
            part = pltpu.roll(tiles_ref[pl.ds(start, 8), :], table_smem[8 + p, chunk], 1)
            tile = jnp.where(lane_group == p, part, tile)
        hat_x, hat_y, hat_z = hat(tile[0:1]), hat(tile[1:2]), hat(tile[2:3])
        plane = jnp.concatenate([hat_y[y : y + 1] * hat_z for y in range(8)], axis=0)
        grad = jnp.where(
            c32 == 0,
            tile[3:4],
            jnp.where(c32 < 10, tile[4:5], jnp.where(c32 < 19, tile[5:6], tile[6:7])),
        )
        grad = grad * basis_rows(tile[7:8], group_sum)
        left = jnp.concatenate(
            [
                jnp.concatenate([grad * hat_x[2 * x + k : 2 * x + k + 1] for x in range(4)], axis=0)
                for k in range(2)
            ],
            axis=1,
        )
        left_high, left_low = split(left)
        high, low = split(plane)
        none = jnp.zeros((64, 128), BF16)

        def both(value):
            return jnp.concatenate(
                [
                    jnp.concatenate([value, none], axis=1),
                    jnp.concatenate([none, value], axis=1),
                ],
                axis=0,
            )

        high, low = both(high), both(low)
        return fast_dot(
            jnp.concatenate([left_high, left_high, left_low], axis=1),
            jnp.concatenate([high, low, high], axis=1),
            NT,
        )

    def several(turn, carry):
        parts = [one(turn * UNROLL + k) for k in range(UNROLL)]
        for k in range(UNROLL):
            b = table_smem[16, turn * UNROLL + k]
            rows = pl.ds(pl.multiple_of(b * 128, 128), 128)
            total_ref[rows, :] += parts[k]
        return carry

    lax.fori_loop(0, (table_smem[17, 0] + UNROLL - 1) // UNROLL, several, 0)

    for c in range(COEF):
        for x in range(4):
            out_ref[c, :, x * 128 : x * 128 + 128] = total_ref[
                pl.ds(x * 32 + c, BRICKS, stride=128), :
            ]


def gradient(tiles, grads):
    return pl.pallas_call(
        gradient_kernel,
        out_shape=jax.ShapeDtypeStruct((COEF, BRICKS, VOXELS), F32),
        in_specs=[ANY, VMEM],
        out_specs=VMEM,
        scratch_shapes=[
            pltpu.VMEM((ALL_CHUNKS * 8 + 8, 128), F32),
            pltpu.VMEM((24, TABLE), I32),
            pltpu.SMEM((24, TABLE), I32),
            pltpu.VMEM((4, ALL_CHUNKS, 128), F32),
            pltpu.VMEM((BRICKS * 128, 128), F32),
            pltpu.SemaphoreType.DMA((2,)),
        ],
        compiler_params=pltpu.CompilerParams(vmem_limit_bytes=48 << 20),
        name="gradient",
    )(tiles, grads)


def local(
    bricks, requests, seg_owner, seg_slot, sample_cells, sample_fracs,
    ray_angles, ray_step, pixel_target,
):
    got, choice = dispatch(
        seg_owner.reshape(1, RAYS),
        seg_slot.reshape(1, RAYS),
        requests.reshape(OWNERS, 2),
        sample_cells.reshape(SAMP, RAYS),
        sample_fracs.reshape(3 * SAMP, RAYS),
        ray_angles,
        ray_step.reshape(1, RAYS),
    )
    tiles, sums = forward(bricks, got)
    colour, tiles, grads = exchange(sums, tiles, choice, pixel_target)
    gradients = gradient(
        tiles.reshape(ALL_CHUNKS * 8, 128), grads.reshape(GROUPS * 8, 128)
    )
    return gradients, colour


def solution(mesh):
    return jax.shard_map(
        local,
        mesh=mesh,
        in_specs=(
            P(None, "seg", None),
            P("seg", "grp", None, None),
            P("seg", "grp", None),
            P("seg", "grp"),
            P(None, "seg", "grp"),
            P(None, None, "seg", "grp"),
            P(None, "grp"),
            P("grp"),
            P(None, "grp"),
        ),
        out_specs=(P(None, "seg", None), P(None, "grp")),
        check_vma=False,
    )
```

time: 926 us -> 146 us (0.16)
  the two profiles are of different devices: /device:TPU:1 before, /device:TPU:12 now
where the time goes in v1:
time: 146 us
  Pallas kernels  137 us (94%)
  local copies, waits for them, and re-layouts  7.44 us (5%)
    pallas_call x1, Pallas kernels, gradient(): pl.pallas_call(gradient_kernel, out_shape=jax.ShapeDtypeStruct((COEF, BRI...  73.5 us
    pallas_call x1, Pallas kernels, exchange(): pl.pallas_call(composite_kernel, out_shape=(jax.ShapeDtypeStruct((3, RAYS...  37.6 us
    pallas_call x1, Pallas kernels, dispatch(): pl.pallas_call(dispatch_kernel, out_shape=(jax.ShapeDtypeStruct((OWNERS,...  15.5 us
    pallas_call x1, Pallas kernels, forward(): pl.pallas_call(forward_kernel, out_shape=(jax.ShapeDtypeStruct((CHUNKS *...  10.8 us
    unnamed x17, local copies, waits for them, and re-layouts  6.67 us

profile of v1, /device:TPU:12, one launch (start us, length us, event | category | flops | bytes accessed | tf_op | source)
XLA Modules:
  0.0 145.6 jit_solution(8249932232830479041)
XLA Ops:
  0.6 0.8 copy.11.wanted_ref
  1.4 0.0 copy-start.1
  1.4 0.7 copy-done.1
  2.1 0.0 copy-start.2
  2.1 0.7 copy-done.2
  2.8 0.0 copy-start.4
  2.8 0.7 copy-done.4
  3.5 0.0 copy-start.5
  3.5 0.7 copy-done.5
  4.2 0.0 copy-start.6
  4.2 0.7 copy-done.6
  4.8 0.0 copy-start.7
  4.8 0.7 copy-done.7
  5.5 15.5 %dispatch.1 = (f32[64,2,128]{2,1,0:T(2,128)S(1)}, f32[64,512]{1,0:T(8,128)S(1)}) custom-call(s32[1,128]{1,0:T(1,128)S(1)} %bitcast.11, s32[1,128]{1,0:T(1,128)S(1)} %copy-done.6, s32[64,2]{1,0:T(8,128)S(1)} %copy.11.wanted_ref, s32[16,128]{1,0:T(8,128)S(1)} %bitcast.10, f32[48,128]{1,0:T(8,128)S(1)} %bitcast.9, f32[2,128]{1,0:T(2,128)S(1)} %copy-done.4, ...), custom_call_target="tpu_custom_call" | custom-call | tf_op jit(solution)/shard_map/dispatch/pallas_call | solution.py:188
  21.0 0.0 copy-start
  21.0 1.3 copy-done
  22.4 10.8 %interpolate.1 = (f32[256,128]{1,0:T(8,128)S(1)}, f32[32,1,128]{2,1,0:T(1,128)S(1)}) custom-call(bf16[28,48,512]{2,1,0:T(8,128)(2,1)S(1)} %copy-done, f32[64,2,128]{2,1,0:T(2,128)S(1)} %get-tuple-element.9.got_ref), custom_call_target="tpu_custom_call" | custom-call | tf_op jit(solution)/shard_map/interpolate/pallas_call | solution.py:318
  33.2 0.0 copy-start.3
  33.2 0.7 copy-done.3
  33.9 37.6 %composite.1 = (f32[3,128]{1,0:T(4,128)S(1)}, f32[8,256,128]{2,1,0:T(8,128)S(1)}, f32[8,8,128]{2,1,0:T(8,128)S(1)}) custom-call(f32[32,1,128]{2,1,0:T(1,128)S(1)} %get-tuple-element.10.sums_ref, f32[256,128]{1,0:T(8,128)S(1)} %get-tuple-element.11.tiles_ref, f32[64,512]{1,0:T(8,128)S(1)} %get-tuple-element.12.choice_ref, f32[3,128]{1,0:T(4,128)S(1)} %copy-done.3), custom_call_target="tpu_custom_call" | custom-call | tf_op jit(solution)/shard_map/composite/pallas_call | solution.py:440
  71.5 73.5 %gradient.1 = f32[28,48,512]{2,1,0:T(8,128)} custom-call(f32[2048,128]{1,0:T(8,128)S(1)} %bitcast.7, f32[64,128]{1,0:T(8,128)S(1)} %bitcast.8), custom_call_target="tpu_custom_call" | custom-call | tf_op jit(solution)/shard_map/gradient/pallas_call | solution.py:624
  145.0 0.6 copy.13
Async XLA Ops:
  1.4 0.7 copy-start.1
  2.1 0.7 copy-start.2
  2.8 0.7 copy-start.4
  3.5 0.7 copy-start.5
  4.2 0.7 copy-start.6
  4.8 0.7 copy-start.7
  21.0 1.3 copy-start
  33.2 0.7 copy-start.3

commit v2 on v1

v2 whole, which is shorter than its diff:
```python
import functools

import jax
import jax.numpy as jnp
from jax import lax
from jax.experimental import pallas as pl
from jax.experimental.pallas import tpu as pltpu
from jax.sharding import PartitionSpec as P

COEF = 28
VOXELS = 512
SAMP = 16
OWNERS = 64
GROUPS = 8
SLOTS = 4
BRICKS = 48
RAYS = 128
CHUNKS = OWNERS * SLOTS // 8
ALL_CHUNKS = GROUPS * CHUNKS
TABLE = 384
UNROLL = 16
FUNROLL = 8
LOSS_SCALE = 1024.0
BASIS_0 = 0.28209479
ROW_OF = [24] + [
    25 + ch if k == 0 else ch * 8 + k - 1 for ch in range(3) for k in range(9)
]
F32 = jnp.float32
BF16 = jnp.bfloat16
I32 = jnp.int32
VMEM = pl.BlockSpec(memory_space=pltpu.VMEM)
ANY = pl.BlockSpec(memory_space=pl.ANY)
MESH = pl.DeviceIdType.MESH
NN = (((1,), (0,)), ((), ()))
NT = (((1,), (1,)), ((), ()))


def iota(shape, dim):
    return lax.broadcasted_iota(I32, shape, dim)


def exact_dot(a, b, dims=NN):
    return lax.dot_general(
        a, b, dims, precision=lax.Precision.HIGHEST, preferred_element_type=F32
    )


def fast_dot(a, b, dims=NN):
    return lax.dot_general(a, b, dims, preferred_element_type=F32)


def split(value):
    high = value.astype(BF16)
    return high, (value - high.astype(F32)).astype(BF16)


def hat(place):
    return jnp.maximum(1.0 - jnp.abs(place - iota((8, 128), 0).astype(F32)), 0.0)


def softplus(value):
    return jnp.maximum(value, 0.0) + jnp.log1p(jnp.exp(-jnp.abs(value)))


def sigmoid(value):
    return 1.0 / (1.0 + jnp.exp(-value))


def ray_basis(angles):
    polar = angles[0:1]
    azimuth = angles[1:2]
    x = jnp.sin(polar) * jnp.cos(azimuth)
    y = jnp.sin(polar) * jnp.sin(azimuth)
    z = jnp.cos(polar)
    return [
        BASIS_0 * jnp.ones_like(x),
        -0.48860251 * y,
        0.48860251 * z,
        -0.48860251 * x,
        1.09254843 * x * y,
        -1.09254843 * y * z,
        0.31539157 * (2.0 * z * z - x * x - y * y),
        -1.09254843 * x * z,
        0.54627422 * (x * x - y * y),
    ]


def pack(owner, slot, wanted, cells, fracs, basis, step):
    mine = owner == iota((OWNERS, RAYS), 0)
    across = jnp.broadcast_to(owner, (RAYS, RAYS))
    ahead = iota((RAYS, RAYS), 0) < iota((RAYS, RAYS), 1)
    rank = jnp.sum(
        jnp.where((jnp.transpose(across) == across) & ahead, 1, 0), axis=0, keepdims=True
    )
    columns = jnp.transpose(wanted)
    brick = jnp.sum(
        jnp.where(mine, jnp.where(slot == 0, columns[:, 0:1], columns[:, 1:2]), 0),
        axis=0, keepdims=True,
    )
    chosen = [mine & (rank == j) for j in range(SLOTS)]
    choice = jnp.concatenate([jnp.where(one, 1.0, 0.0) for one in chosen], axis=1)
    lane = iota((OWNERS, RAYS), 1)
    bricks = jnp.zeros((OWNERS, RAYS), I32)
    for j in range(SLOTS):
        named = jnp.sum(jnp.where(chosen[j], brick, 0), axis=1, keepdims=True)
        bricks = jnp.where(lane == j, named, bricks)
    cell_x = (cells * 1338) >> 16
    rest = cells - cell_x * 49
    cell_y = (rest * 9363) >> 16
    cell_z = rest - cell_y * 7
    place_x = cell_x.astype(F32) + fracs[0:16]
    place_y = cell_y.astype(F32) + fracs[16:32]
    place_z = cell_z.astype(F32) + fracs[32:48]
    row = iota((SAMP, RAYS), 0)
    extra = jnp.where(row == 11, 1.0, 0.0)
    for k, value in enumerate(basis + [step, brick.astype(F32) + 1.0]):
        extra = jnp.where(row == k, value, extra)
    none = jnp.zeros((SAMP, RAYS), F32)

    def placed(first, second):
        parts = []
        for j in range(SLOTS):
            rows = [none] * 8
            rows[j] = first
            rows[4 + j] = second
            parts.append(jnp.concatenate(rows, axis=0))
        return jnp.concatenate(parts, axis=1)

    return (
        choice,
        bricks,
        exact_dot(choice, placed(place_x, place_y), NT),
        exact_dot(choice, placed(place_z, extra), NT),
    )


def greet(axes):
    barrier = pltpu.get_barrier_semaphore()
    total = 0
    for axis, count in axes:
        me = lax.axis_index(axis)

        def hail(turn, carry, axis=axis, count=count, me=me):
            pl.semaphore_signal(
                barrier,
                inc=1,
                device_id={axis: lax.rem(me + turn, count)},
                device_id_type=MESH,
            )
            return carry

        lax.fori_loop(1, count, hail, 0)
        total += count - 1
    return lambda: pl.semaphore_wait(barrier, total)


def send_all(axis, count, source, target, send_sem, recv_sem):
    me = lax.axis_index(axis)

    def one(turn, carry):
        peer = lax.rem(me + turn, count)
        pltpu.make_async_remote_copy(
            src_ref=source(peer),
            dst_ref=target.at[me],
            send_sem=send_sem,
            recv_sem=recv_sem,
            device_id={axis: peer},
            device_id_type=MESH,
        ).start()
        return carry

    lax.fori_loop(1, count, one, 0)


def wait_all(target, count, sem):
    part = target.at[pl.ds(0, count - 1)]
    pltpu.make_async_copy(part, part, sem).wait()


def lay_out_bricks(bricks_ref, wide_ref, brick_ref):
    for c in range(COEF, 32):
        for x in range(4):
            wide_ref[x, pl.ds(c, BRICKS, stride=32), :] = jnp.zeros((BRICKS, 128), F32)
    for c in range(COEF):
        for x in range(4):
            wide_ref[x, pl.ds(ROW_OF[c], BRICKS, stride=32), :] = bricks_ref[
                c, :, x * 128 : x * 128 + 128
            ].astype(F32)

    def narrow(turn, carry):
        for k in range(8):
            rows = pl.ds(pl.multiple_of(turn * 256 + k * 32, 32), 32)
            for x in range(4):
                brick_ref[turn * 8 + k, :, x * 128 : x * 128 + 128] = wide_ref[
                    x, rows, :
                ].astype(BF16)
        return carry

    lax.fori_loop(0, BRICKS // 8, narrow, 0)


def unpack(got_ref, half_ref, place_ref, basis_ref):
    left = iota((CHUNKS, 128), 1) < 64
    for half in range(2):
        half_ref[...] = got_ref[:, half, :]
        even = half_ref[pl.ds(0, CHUNKS, stride=2), :]
        odd = half_ref[pl.ds(1, CHUNKS, stride=2), :]
        place_ref[2 * half] = jnp.where(left, even, pltpu.roll(odd, 64, 1))
        place_ref[2 * half + 1] = jnp.where(left, pltpu.roll(even, 64, 1), odd)
    row, lane = iota((128, 1024), 0), iota((128, 1024), 1)
    spread = jnp.where(row == ((lane % 128) // 16) * 16 + lane // 128 + 1, 1.0, 0.0)
    basis = exact_dot(place_ref[3], spread)
    for k in range(8):
        basis_ref[pl.ds(k, CHUNKS, stride=8), :] = basis[:, k * 128 : k * 128 + 128]


def interpolate(brick_ref, place_ref, basis_ref, id_smem, raw_ref):
    lane_group = iota((32, 128), 1) // 16

    def one(chunk):
        hat_x = hat(place_ref[0, pl.ds(chunk, 1), :])
        hat_y = hat(place_ref[1, pl.ds(chunk, 1), :])
        hat_z = hat(place_ref[2, pl.ds(chunk, 1), :])
        plane = jnp.concatenate([hat_y[y : y + 1] * hat_z for y in range(8)], axis=0)
        weights = jnp.concatenate([hat_x[x : x + 1] * plane for x in range(8)], axis=0)
        high, low = split(weights)
        rows = []
        for seg in range(8):
            b = id_smem[chunk * 2 + seg // 4, 0, seg % 4]
            rows.append(brick_ref[b])
        values = fast_dot(
            jnp.concatenate(rows, axis=0), jnp.concatenate([high, low], axis=1)
        )
        coef = jnp.zeros((32, 128), F32)
        for seg in range(8):
            part = values[seg * 32 : seg * 32 + 32]
            coef = jnp.where(lane_group == seg, part[:, 0:128] + part[:, 128:256], coef)
        basis = basis_ref[pl.ds(pl.multiple_of(chunk * 8, 8), 8), :]
        raw_ref[0, pl.ds(chunk, 1), :] = coef[24:25]
        for ch in range(3):
            raw_ref[1 + ch, pl.ds(chunk, 1), :] = coef[25 + ch : 26 + ch] * BASIS_0 + jnp.sum(
                coef[8 * ch : 8 * ch + 8] * basis, axis=0, keepdims=True
            )

    def several(turn, carry):
        for k in range(FUNROLL):
            one(turn * FUNROLL + k)
        return carry

    lax.fori_loop(0, CHUNKS // FUNROLL, several, 0)


def segment_sums(raw_ref, extra):
    optical, through, opaque, _ = march(raw_ref[0], extra)
    light = through * opaque
    total = jnp.zeros((CHUNKS, 128), F32)
    row, lane = iota((128, 128), 0), iota((128, 128), 1)
    for v in range(4):
        part = optical if v == 3 else light * sigmoid(raw_ref[1 + v])
        total += exact_dot(part, jnp.where(lane == (row // 16) * 8 + v, 1.0, 0.0))
    return total


def march(density, extra):
    row, lane = iota((128, 128), 0), iota((128, 128), 1)
    same = row // 16 == lane // 16
    step = exact_dot(extra, jnp.where(same & (row % 16 == 9), 1.0, 0.0))
    optical = softplus(density) * step
    before = exact_dot(optical, jnp.where(same & (row < lane), 1.0, 0.0))
    through = jnp.exp(-before)
    remains = jnp.exp(-optical)
    return optical, through, 1.0 - remains, (step, remains)


def to_rays(sums, choice):
    half = lax.rem(lax.axis_index("seg"), 2)
    turned = pltpu.roll(sums, lax.rem(128 - half * 32, 128), 1)
    found = exact_dot(jnp.transpose(turned)[0:32], choice)
    total = jnp.zeros((8, RAYS), F32)
    for j in range(SLOTS):
        total += found[8 * j : 8 * j + 8, RAYS * j : RAYS * j + RAYS]
    return total


def composite(colours, taus, target):
    me = lax.axis_index("seg")
    lower = jnp.where(iota((OWNERS, OWNERS), 1) < iota((OWNERS, OWNERS), 0), 1.0, 0.0)
    through = jnp.exp(-exact_dot(lower, taus))
    depth = iota((OWNERS, RAYS), 0)
    here = jnp.sum(jnp.where(depth == me, through, 0.0), axis=0, keepdims=True)
    colour, grad_colour = [], []
    grad_tau = jnp.zeros((1, RAYS), F32)
    for v in range(3):
        contrib = through * colours[v]
        colour.append(jnp.sum(contrib, axis=0, keepdims=True))
        behind = jnp.sum(jnp.where(depth > me, contrib, 0.0), axis=0, keepdims=True)
        misfit = LOSS_SCALE * (colour[v] - target[v : v + 1])
        grad_colour.append(here * misfit)
        grad_tau -= misfit * behind
    return colour, grad_colour + [grad_tau]


def to_slots(grads, choice):
    me = lax.axis_index("seg")
    row = iota((SLOTS * 4, RAYS), 0)
    block = jnp.zeros((SLOTS * 4, RAYS), F32)
    for v in range(4):
        block = jnp.where(row % 4 == v, grads[v], block)
    wide = jnp.concatenate(
        [jnp.where(row // 4 == j, block, 0.0) for j in range(SLOTS)], axis=1
    )
    wide = jnp.concatenate([wide, jnp.zeros((112, SLOTS * RAYS), F32)], axis=0)
    placed = exact_dot(choice, wide, NT)
    return pltpu.roll(placed, (me // 16) * 32 + lax.rem(me, 2) * 16, 1)


def render_kernel(
    owner_hbm, slot_hbm, wanted_hbm, cells_hbm, fracs_hbm, angles_hbm, step_hbm, target_hbm,
    bricks_hbm,
    colour_ref, places_ref, raws_ref, all_grads_ref,
    owner_ref, slot_ref, wanted_ref, cells_ref, fracs_ref, angles_ref, step_ref, target_ref,
    bricks_ref,
    choice_ref, out_ref, got_ref, wide_ref, brick_ref, half_ref, numbers_ref, ids_ref, id_smem,
    place_ref, raw_ref, basis_ref,
    sums_ref, back_ref, ray_ref, rays_ref, slot_out_ref, slots_ref, grads_ref,
    load_sems, send_sems, recv_sems, own_sems,
):
    loads = [
        pltpu.make_async_copy(source, target, load_sems.at[k])
        for k, (source, target) in enumerate(
            [
                (owner_hbm, owner_ref), (slot_hbm, slot_ref), (wanted_hbm, wanted_ref),
                (cells_hbm, cells_ref), (fracs_hbm, fracs_ref), (angles_hbm, angles_ref),
                (step_hbm, step_ref), (target_hbm, target_ref), (bricks_hbm, bricks_ref),
            ]
        )
    ]
    for load in loads:
        load.start()
    met = greet([("seg", OWNERS), ("grp", GROUPS)])
    for load in loads[:8]:
        load.wait()
    me = lax.axis_index("seg")
    group = lax.axis_index("grp")

    choice, numbers, first, second = pack(
        owner_ref[...], slot_ref[...], wanted_ref[...], cells_ref[...], fracs_ref[...],
        ray_basis(angles_ref[...]), step_ref[...],
    )
    choice_ref[...] = choice
    out_ref[:, 0, :] = first
    out_ref[:, 1, :] = second
    numbers_ref[:, 0, :] = numbers
    met()
    send_all(
        "seg", OWNERS, lambda peer: numbers_ref.at[peer], ids_ref, send_sems.at[7], recv_sems.at[7]
    )
    ids_ref[me] = numbers_ref[me]
    send_all(
        "seg", OWNERS, lambda peer: out_ref.at[peer], got_ref, send_sems.at[0], recv_sems.at[0]
    )
    got_ref[me] = out_ref[me]
    loads[8].wait()
    lay_out_bricks(bricks_ref, wide_ref, brick_ref)
    wait_all(got_ref, OWNERS, recv_sems.at[0])

    unpack(got_ref, half_ref, place_ref, basis_ref)
    extra = place_ref[3]
    send_all(
        "grp", GROUPS, lambda peer: place_ref, places_ref, send_sems.at[1], recv_sems.at[1]
    )
    own_places = pltpu.make_async_copy(place_ref, places_ref.at[group], own_sems.at[0])
    own_places.start()
    wait_all(ids_ref, OWNERS, recv_sems.at[7])
    ids = pltpu.make_async_copy(ids_ref, id_smem, own_sems.at[2])
    ids.start()
    ids.wait()
    interpolate(brick_ref, place_ref, basis_ref, id_smem, raw_ref)
    sums_ref[:, 0, :] = segment_sums(raw_ref, extra)

    send_all(
        "seg", OWNERS, lambda peer: sums_ref.at[peer // 2], back_ref,
        send_sems.at[2], recv_sems.at[2],
    )
    back_ref[me] = sums_ref[me // 2]
    send_all("grp", GROUPS, lambda peer: raw_ref, raws_ref, send_sems.at[3], recv_sems.at[3])
    own_raws = pltpu.make_async_copy(raw_ref, raws_ref.at[group], own_sems.at[1])
    own_raws.start()
    wait_all(back_ref, OWNERS, recv_sems.at[2])
    choice = choice_ref[...]
    ray_ref[...] = to_rays(back_ref[:, 0, :], choice)[0:4]

    send_all("seg", OWNERS, lambda peer: ray_ref, rays_ref, send_sems.at[4], recv_sems.at[4])
    rays_ref[me] = ray_ref[...]
    wait_all(rays_ref, OWNERS, recv_sems.at[4])
    colour, grads = composite(
        [rays_ref[:, v, :] for v in range(3)], rays_ref[:, 3, :], target_ref[...]
    )
    for v in range(3):
        colour_ref[v : v + 1, :] = colour[v]
    slot_out_ref[:, 0, :] = to_slots(grads, choice)

    send_all(
        "seg", OWNERS, lambda peer: slot_out_ref.at[peer], slots_ref,
        send_sems.at[5], recv_sems.at[5],
    )
    slots_ref[me] = slot_out_ref[me]
    wait_all(slots_ref, OWNERS, recv_sems.at[5])
    pick = jnp.where((iota((8, OWNERS), 1) // 2) % 8 == iota((8, OWNERS), 0), 1.0, 0.0)
    grads_ref[...] = exact_dot(pick, slots_ref[:, 0, :])
    send_all(
        "grp", GROUPS, lambda peer: grads_ref, all_grads_ref, send_sems.at[6], recv_sems.at[6]
    )
    all_grads_ref[group] = grads_ref[...]
    wait_all(all_grads_ref, GROUPS, recv_sems.at[6])
    own_places.wait()
    own_raws.wait()
    wait_all(places_ref, GROUPS, recv_sems.at[1])
    wait_all(raws_ref, GROUPS, recv_sems.at[3])
    wait_all(got_ref, OWNERS, send_sems.at[0])
    wait_all(ids_ref, OWNERS, send_sems.at[7])
    wait_all(places_ref, GROUPS, send_sems.at[1])
    wait_all(back_ref, OWNERS, send_sems.at[2])
    wait_all(raws_ref, GROUPS, send_sems.at[3])
    wait_all(rays_ref, OWNERS, send_sems.at[4])
    wait_all(slots_ref, OWNERS, send_sems.at[5])
    wait_all(all_grads_ref, GROUPS, send_sems.at[6])


def render(*operands):
    return pl.pallas_call(
        render_kernel,
        out_shape=(
            jax.ShapeDtypeStruct((3, RAYS), F32),
            jax.ShapeDtypeStruct((GROUPS, 4, CHUNKS, 128), F32),
            jax.ShapeDtypeStruct((GROUPS, 4, CHUNKS, 128), F32),
            jax.ShapeDtypeStruct((GROUPS, 8, 128), F32),
        ),
        in_specs=[ANY] * 9,
        out_specs=(VMEM, ANY, ANY, VMEM),
        scratch_shapes=[pltpu.VMEM(x.shape, x.dtype) for x in operands]
        + [
            pltpu.VMEM((OWNERS, SLOTS * RAYS), F32),
            pltpu.VMEM((OWNERS, 2, 128), F32),
            pltpu.VMEM((OWNERS, 2, 128), F32),
            pltpu.VMEM((4, BRICKS * 32, 128), F32),
            pltpu.VMEM((BRICKS, 32, VOXELS), BF16),
            pltpu.VMEM((OWNERS, 128), F32),
            pltpu.VMEM((OWNERS, 1, 128), I32),
            pltpu.VMEM((OWNERS, 1, 128), I32),
            pltpu.SMEM((OWNERS, 1, 128), I32),
            pltpu.VMEM((4, CHUNKS, 128), F32),
            pltpu.VMEM((4, CHUNKS, 128), F32),
            pltpu.VMEM((CHUNKS * 8, 128), F32),
            pltpu.VMEM((CHUNKS, 1, 128), F32),
            pltpu.VMEM((OWNERS, 1, 128), F32),
            pltpu.VMEM((4, RAYS), F32),
            pltpu.VMEM((OWNERS, 4, RAYS), F32),
            pltpu.VMEM((OWNERS, 1, 128), F32),
            pltpu.VMEM((OWNERS, 1, 128), F32),
            pltpu.VMEM((8, 128), F32),
            pltpu.SemaphoreType.DMA((9,)),
            pltpu.SemaphoreType.DMA((8,)),
            pltpu.SemaphoreType.DMA((8,)),
            pltpu.SemaphoreType.DMA((3,)),
        ],
        compiler_params=pltpu.CompilerParams(
            collective_id=0, has_side_effects=True, vmem_limit_bytes=64 << 20
        ),
        name="render",
    )(*operands)


def plan_chunks(extra):
    across = jnp.transpose(extra)
    named = iota((64, ALL_CHUNKS), 0).astype(F32) + 1.0
    hits = [
        jnp.where(across[seg * 16 + 10 : seg * 16 + 11] == named, 1.0, 0.0) for seg in range(8)
    ]
    earlier = jnp.where(
        iota((ALL_CHUNKS, ALL_CHUNKS), 0) < iota((ALL_CHUNKS, ALL_CHUNKS), 1), 1.0, 0.0
    ).astype(BF16)
    counts = fast_dot(jnp.concatenate(hits, axis=0).astype(BF16), earlier)
    carry = jnp.zeros((64, 1), F32)
    ranks = []
    for seg in range(8):
        ranks.append(counts[seg * 64 : seg * 64 + 64] + carry)
        carry = carry + jnp.sum(hits[seg], axis=1, keepdims=True)
    full = jnp.floor((carry + 7.0) * 0.125)
    lower = jnp.where(iota((64, 64), 1) < iota((64, 64), 0), 1.0, 0.0).astype(BF16)
    full_wide = jnp.broadcast_to(full, (64, 128))
    start = fast_dot(lower, full_wide.astype(BF16))
    end = start + full_wide
    start256 = jnp.concatenate([start, start], axis=1)
    selectors, values = [], []
    row = iota((32, ALL_CHUNKS), 0)
    lane = iota((32, ALL_CHUNKS), 1).astype(F32)
    for seg in range(8):
        place = (
            jnp.sum(hits[seg] * (8.0 * start256 + ranks[seg] + 1.0), axis=0, keepdims=True) - 1.0
        )
        chunk = jnp.floor(place * 0.125)
        inside = place - 8.0 * chunk
        selectors.append(
            jnp.where(iota((TABLE, ALL_CHUNKS), 0).astype(F32) == chunk, 1.0, 0.0).astype(BF16)
        )
        kind = jnp.where(
            row < 8, lane, jnp.where(row < 16, float(seg), jnp.where(row < 24, 1.0, 0.0))
        )
        values.append(jnp.where((row % 8).astype(F32) == inside, kind, 0.0).astype(BF16))
    table = fast_dot(
        jnp.concatenate(values, axis=1), jnp.concatenate(selectors, axis=1), NT
    )
    tile = table[0:8] + (1.0 - table[16:24]) * float(ALL_CHUNKS)
    turn = 16.0 * (iota((8, TABLE), 0).astype(F32) - table[8:16])
    turn = jnp.where(turn < 0.0, turn + 128.0, turn)
    place = iota((64, 128), 1).astype(F32)
    real = iota((64, 128), 0) < BRICKS
    owner = [
        jnp.sum(jnp.where((end <= place + 128.0 * k) & real, 1.0, 0.0), axis=0, keepdims=True)
        for k in range(TABLE // 128)
    ]
    owner = jnp.minimum(jnp.concatenate(owner, axis=1), float(BRICKS - 1))
    number = jnp.sum(full_wide, axis=0, keepdims=True)
    number = jnp.concatenate([number] * (TABLE // 128), axis=1)
    last = jnp.where(iota((8, TABLE), 0) == 0, owner, number)
    return jnp.concatenate([tile, turn, last], axis=0).astype(I32)


def gradient_kernel(
    places_hbm, raws_hbm, grads_hbm, colour_hbm, out_ref, colour_ref,
    places_ref, raws_ref, grads_ref, tiles_ref, table_vmem, table_smem, slot_ref, total_ref, sems,
):
    load_places = pltpu.make_async_copy(places_hbm, places_ref, sems.at[0])
    load_raws = pltpu.make_async_copy(raws_hbm, raws_ref, sems.at[2])
    load_places.start()
    load_raws.start()
    load_grads = pltpu.make_async_copy(grads_hbm, grads_ref, sems.at[3])
    load_grads.start()
    load_colour = pltpu.make_async_copy(colour_hbm, colour_ref, sems.at[4])
    load_colour.start()
    tiles_ref[pl.ds(ALL_CHUNKS * 8, 8), :] = jnp.zeros((8, 128), F32)
    total_ref[...] = jnp.zeros_like(total_ref)
    load_places.wait()
    extra = jnp.concatenate([places_ref[g, 3] for g in range(GROUPS)], axis=0)
    table_vmem[...] = plan_chunks(extra)
    plan = pltpu.make_async_copy(table_vmem, table_smem, sems.at[1])
    plan.start()
    for g in range(GROUPS):
        for q in range(4):
            tiles_ref[pl.ds(g * CHUNKS * 8 + 4 + q, CHUNKS, stride=8), :] = places_ref[g, q]

    load_grads.wait()
    load_colour.wait()
    row, lane = iota((128, 128), 0), iota((128, 128), 1)
    for part in range(4):
        for v in range(4):
            spread = jnp.where(row == part * 32 + (lane // 16) * 4 + v, 1.0, 0.0)
            wide = exact_dot(grads_ref[...], spread)
            for g in range(GROUPS):
                slot_ref[v, pl.ds(g * CHUNKS + part * 8, 8), :] = wide[g * 8 : g * 8 + 8]
    load_raws.wait()

    def raw(v):
        return jnp.concatenate([raws_ref[g, v] for g in range(GROUPS)], axis=0)

    density = raw(0)
    optical, through, opaque, (step, remains) = march(density, extra)
    light = through * opaque
    mixed = jnp.zeros((ALL_CHUNKS, 128), F32)
    for v in range(3):
        radiance = sigmoid(raw(1 + v))
        grad_colour = slot_ref[v]
        mixed += grad_colour * radiance
        tiles_ref[pl.ds(1 + v, ALL_CHUNKS, stride=8), :] = (
            grad_colour * light * radiance * (1.0 - radiance)
        )
    later = jnp.where((row // 16 == lane // 16) & (row > lane), 1.0, 0.0)
    grad_optical = through * remains * mixed - exact_dot(light * mixed, later) + slot_ref[3]
    tiles_ref[pl.ds(0, ALL_CHUNKS, stride=8), :] = grad_optical * step * sigmoid(density)
    plan.wait()

    lane_group = iota((8, 128), 1) // 16
    pick = lane_group * 16 + iota((8, 128), 0) + 1
    row8 = iota((8, 128), 0)
    first = jnp.where(row8 == 0, 1.0, jnp.where(row8 < 4, BASIS_0, 0.0))

    def one(chunk):
        tile = jnp.zeros((8, 128), F32)
        for p in range(8):
            start = pl.multiple_of(table_smem[p, chunk] * 8, 8)
            part = pltpu.roll(tiles_ref[pl.ds(start, 8), :], table_smem[8 + p, chunk], 1)
            tile = jnp.where(lane_group == p, part, tile)
        hat_x, hat_y, hat_z = hat(tile[4:5]), hat(tile[5:6]), hat(tile[6:7])
        plane = jnp.concatenate([hat_y[y : y + 1] * hat_z for y in range(8)], axis=0)
        basis = jnp.take_along_axis(jnp.broadcast_to(tile[7:8], (8, 128)), pick, axis=1)
        grad = jnp.concatenate([basis * tile[ch : ch + 1] for ch in (1, 2, 3)] + [tile * first], axis=0)
        left = jnp.concatenate(
            [
                jnp.concatenate([grad * hat_x[2 * x + k : 2 * x + k + 1] for x in range(4)], axis=0)
                for k in range(2)
            ],
            axis=1,
        )
        left_high, left_low = split(left)
        high, low = split(plane)
        none = jnp.zeros((64, 128), BF16)

        def both(value):
            return jnp.concatenate(
                [
                    jnp.concatenate([value, none], axis=1),
                    jnp.concatenate([none, value], axis=1),
                ],
                axis=0,
            )

        high, low = both(high), both(low)
        return fast_dot(
            jnp.concatenate([left_high, left_high, left_low], axis=1),
            jnp.concatenate([high, low, high], axis=1),
            NT,
        )

    def several(turn, carry):
        parts = [one(turn * UNROLL + k) for k in range(UNROLL)]
        for k in range(UNROLL):
            b = table_smem[16, turn * UNROLL + k]
            rows = pl.ds(pl.multiple_of(b * 128, 128), 128)
            total_ref[rows, :] += parts[k]
        return carry

    lax.fori_loop(0, (table_smem[17, 0] + UNROLL - 1) // UNROLL, several, 0)

    for c in range(COEF):
        for x in range(4):
            out_ref[c, :, x * 128 : x * 128 + 128] = total_ref[
                pl.ds(x * 32 + ROW_OF[c], BRICKS, stride=128), :
            ]


def gradient(places, raws, grads, colour):
    return pl.pallas_call(
        gradient_kernel,
        out_shape=(
            jax.ShapeDtypeStruct((COEF, BRICKS, VOXELS), F32),
            jax.ShapeDtypeStruct((3, RAYS), F32),
        ),
        in_specs=[ANY] * 4,
        out_specs=(VMEM, VMEM),
        scratch_shapes=[
            pltpu.VMEM((GROUPS, 4, CHUNKS, 128), F32),
            pltpu.VMEM((GROUPS, 4, CHUNKS, 128), F32),
            pltpu.VMEM((GROUPS * 8, 128), F32),
            pltpu.VMEM((ALL_CHUNKS * 8 + 8, 128), F32),
            pltpu.VMEM((24, TABLE), I32),
            pltpu.SMEM((24, TABLE), I32),
            pltpu.VMEM((4, ALL_CHUNKS, 128), F32),
            pltpu.VMEM((BRICKS * 128, 128), F32),
            pltpu.SemaphoreType.DMA((5,)),
        ],
        compiler_params=pltpu.CompilerParams(vmem_limit_bytes=64 << 20),
        name="gradient",
    )(places, raws, grads, colour)


def local(
    bricks, requests, seg_owner, seg_slot, sample_cells, sample_fracs,
    ray_angles, ray_step, pixel_target,
):
    colour, places, raws, grads = render(
        seg_owner.reshape(1, RAYS),
        seg_slot.reshape(1, RAYS),
        jnp.transpose(requests.reshape(OWNERS, 2)),
        sample_cells.reshape(SAMP, RAYS),
        sample_fracs.reshape(3 * SAMP, RAYS),
        ray_angles,
        ray_step.reshape(1, RAYS),
        pixel_target,
        bricks,
    )
    return gradient(places, raws, grads.reshape(GROUPS * 8, 128), colour)


def solution(mesh):
    return jax.shard_map(
        local,
        mesh=mesh,
        in_specs=(
            P(None, "seg", None),
            P("seg", "grp", None, None),
            P("seg", "grp", None),
            P("seg", "grp"),
            P(None, "seg", "grp"),
            P(None, None, "seg", "grp"),
            P(None, "grp"),
            P("grp"),
            P(None, "grp"),
        ),
        out_specs=(P(None, "seg", None), P(None, "grp")),
        check_vma=False,
    )
```

time: 146 us -> 81.6 us (0.56)
  the two profiles are of different devices: /device:TPU:12 before, /device:TPU:20 now
where the time goes in v2:
time: 81.6 us; the launch traced here: 81.5 us
  Pallas kernels  80.9 us (99%)
    pallas_call x1, Pallas kernels, render(): pl.pallas_call(render_kernel, out_shape=(jax.ShapeDtypeStruct((3, RAYS),...  51.4 us
    pallas_call x1, Pallas kernels, gradient(): pl.pallas_call(gradient_kernel, out_shape=(jax.ShapeDtypeStruct((COEF, BR...  29.4 us

profile of v2, /device:TPU:20, one launch (start us, length us, event | category | flops | bytes accessed | tf_op | source)
XLA Modules:
  0.0 81.5 jit_solution(11159425283475401965)
XLA Ops:
  0.6 51.4 %render.1 = (f32[3,128]{1,0:T(4,128)}, f32[8,4,32,128]{3,2,1,0:T(8,128)}, f32[8,4,32,128]{3,2,1,0:T(8,128)}, f32[8,8,128]{2,1,0:T(8,128)}) custom-call(s32[1,128]{1,0:T(1,128)} %bitcast.12, s32[1,128]{1,0:T(1,128)} %slot_hbm.1, s32[2,64]{1,0:T(2,128)} %bitcast.11, s32[16,128]{1,0:T(8,128)} %bitcast.10, f32[48,128]{1,0:T(8,128)} %bitcast.9, ...), custom_call_target="tpu_custom_call" | custom-call | tf_op jit(solution)/shard_map/render/pallas_call | solution.py:431
  52.1 29.4 %gradient.1 = (f32[28,48,512]{2,1,0:T(8,128)}, f32[3,128]{1,0:T(4,128)}) custom-call(f32[8,4,32,128]{3,2,1,0:T(8,128)} %get-tuple-element.6.places_hbm, f32[8,4,32,128]{3,2,1,0:T(8,128)} %get-tuple-element.7.raws_hbm, f32[64,128]{1,0:T(8,128)} %bitcast.8, f32[3,128]{1,0:T(4,128)} %get-tuple-element.9.colour_hbm), custom_call_target="tpu_custom_call" | custom-call | tf_op jit(solution)/shard_map/gradient/pallas_call | solution.py:643

commit v3 on v2

--- a/solution.py
+++ b/solution.py
@@ -18,7 +18,8 @@
 CHUNKS = OWNERS * SLOTS // 8
 ALL_CHUNKS = GROUPS * CHUNKS
 TABLE = 384
-UNROLL = 16
+UNROLL = 32
+BRICK_ROWS = 136
 FUNROLL = 8
 LOSS_SCALE = 1024.0
 BASIS_0 = 0.28209479
@@ -99,7 +100,7 @@
     )
     chosen = [mine & (rank == j) for j in range(SLOTS)]
     choice = jnp.concatenate([jnp.where(one, 1.0, 0.0) for one in chosen], axis=1)
-    lane = iota((OWNERS, RAYS), 1)
+    lane = iota((OWNERS, RAYS), 1) - lax.rem(lax.axis_index("seg"), 32) * SLOTS
     bricks = jnp.zeros((OWNERS, RAYS), I32)
     for j in range(SLOTS):
         named = jnp.sum(jnp.where(chosen[j], brick, 0), axis=1, keepdims=True)
@@ -149,7 +150,7 @@
             )
             return carry
 
-        lax.fori_loop(1, count, hail, 0)
+        lax.fori_loop(1, count, hail, 0, unroll=9 if count == OWNERS else 7)
         total += count - 1
     return lambda: pl.semaphore_wait(barrier, total)
 
@@ -169,7 +170,29 @@
         ).start()
         return carry
 
-    lax.fori_loop(1, count, one, 0)
+    lax.fori_loop(1, count, one, 0, unroll=9 if count == OWNERS else 7)
+
+
+def ring_start(ref, step, send_sems, recv_sems):
+    me = lax.axis_index("grp")
+    for way in range(2 if step < 4 else 1):
+        block = lax.rem(me + GROUPS + (step - 1) * (2 * way - 1), GROUPS)
+        pltpu.make_async_remote_copy(
+            src_ref=ref.at[block],
+            dst_ref=ref.at[block],
+            send_sem=send_sems.at[way, step - 1],
+            recv_sem=recv_sems.at[way, step - 1],
+            device_id={"grp": lax.rem(me + GROUPS + 1 - 2 * way, GROUPS)},
+            device_id_type=MESH,
+        ).start()
+
+
+def ring_wait(ref, step, sems, arriving):
+    me = lax.axis_index("grp")
+    for way in range(2 if step < 4 else 1):
+        away = step if arriving else step - 1
+        part = ref.at[lax.rem(me + GROUPS + away * (2 * way - 1), GROUPS)]
+        pltpu.make_async_copy(part, part, sems.at[way, step - 1]).wait()
 
 
 def wait_all(target, count, sem):
@@ -226,7 +249,7 @@
         high, low = split(weights)
         rows = []
         for seg in range(8):
-            b = id_smem[chunk * 2 + seg // 4, 0, seg % 4]
+            b = id_smem[chunk // 16, lax.rem(chunk, 16) * 8 + seg]
             rows.append(brick_ref[b])
         values = fast_dot(
             jnp.concatenate(rows, axis=0), jnp.concatenate([high, low], axis=1)
@@ -270,205 +293,6 @@
     through = jnp.exp(-before)
     remains = jnp.exp(-optical)
     return optical, through, 1.0 - remains, (step, remains)
-
-
-def to_rays(sums, choice):
-    half = lax.rem(lax.axis_index("seg"), 2)
-    turned = pltpu.roll(sums, lax.rem(128 - half * 32, 128), 1)
-    found = exact_dot(jnp.transpose(turned)[0:32], choice)
-    total = jnp.zeros((8, RAYS), F32)
-    for j in range(SLOTS):
-        total += found[8 * j : 8 * j + 8, RAYS * j : RAYS * j + RAYS]
-    return total
-
-
-def composite(colours, taus, target):
-    me = lax.axis_index("seg")
-    lower = jnp.where(iota((OWNERS, OWNERS), 1) < iota((OWNERS, OWNERS), 0), 1.0, 0.0)
-    through = jnp.exp(-exact_dot(lower, taus))
-    depth = iota((OWNERS, RAYS), 0)
-    here = jnp.sum(jnp.where(depth == me, through, 0.0), axis=0, keepdims=True)
-    colour, grad_colour = [], []
-    grad_tau = jnp.zeros((1, RAYS), F32)
-    for v in range(3):
-        contrib = through * colours[v]
-        colour.append(jnp.sum(contrib, axis=0, keepdims=True))
-        behind = jnp.sum(jnp.where(depth > me, contrib, 0.0), axis=0, keepdims=True)
-        misfit = LOSS_SCALE * (colour[v] - target[v : v + 1])
-        grad_colour.append(here * misfit)
-        grad_tau -= misfit * behind
-    return colour, grad_colour + [grad_tau]
-
-
-def to_slots(grads, choice):
-    me = lax.axis_index("seg")
-    row = iota((SLOTS * 4, RAYS), 0)
-    block = jnp.zeros((SLOTS * 4, RAYS), F32)
-    for v in range(4):
-        block = jnp.where(row % 4 == v, grads[v], block)
-    wide = jnp.concatenate(
-        [jnp.where(row // 4 == j, block, 0.0) for j in range(SLOTS)], axis=1
-    )
-    wide = jnp.concatenate([wide, jnp.zeros((112, SLOTS * RAYS), F32)], axis=0)
-    placed = exact_dot(choice, wide, NT)
-    return pltpu.roll(placed, (me // 16) * 32 + lax.rem(me, 2) * 16, 1)
-
-
-def render_kernel(
-    owner_hbm, slot_hbm, wanted_hbm, cells_hbm, fracs_hbm, angles_hbm, step_hbm, target_hbm,
-    bricks_hbm,
-    colour_ref, places_ref, raws_ref, all_grads_ref,
-    owner_ref, slot_ref, wanted_ref, cells_ref, fracs_ref, angles_ref, step_ref, target_ref,
-    bricks_ref,
-    choice_ref, out_ref, got_ref, wide_ref, brick_ref, half_ref, numbers_ref, ids_ref, id_smem,
-    place_ref, raw_ref, basis_ref,
-    sums_ref, back_ref, ray_ref, rays_ref, slot_out_ref, slots_ref, grads_ref,
-    load_sems, send_sems, recv_sems, own_sems,
-):
-    loads = [
-        pltpu.make_async_copy(source, target, load_sems.at[k])
-        for k, (source, target) in enumerate(
-            [
-                (owner_hbm, owner_ref), (slot_hbm, slot_ref), (wanted_hbm, wanted_ref),
-                (cells_hbm, cells_ref), (fracs_hbm, fracs_ref), (angles_hbm, angles_ref),
-                (step_hbm, step_ref), (target_hbm, target_ref), (bricks_hbm, bricks_ref),
-            ]
-        )
-    ]
-    for load in loads:
-        load.start()
-    met = greet([("seg", OWNERS), ("grp", GROUPS)])
-    for load in loads[:8]:
-        load.wait()
-    me = lax.axis_index("seg")
-    group = lax.axis_index("grp")
-
-    choice, numbers, first, second = pack(
-        owner_ref[...], slot_ref[...], wanted_ref[...], cells_ref[...], fracs_ref[...],
-        ray_basis(angles_ref[...]), step_ref[...],
-    )
-    choice_ref[...] = choice
-    out_ref[:, 0, :] = first
-    out_ref[:, 1, :] = second
-    numbers_ref[:, 0, :] = numbers
-    met()
-    send_all(
-        "seg", OWNERS, lambda peer: numbers_ref.at[peer], ids_ref, send_sems.at[7], recv_sems.at[7]
-    )
-    ids_ref[me] = numbers_ref[me]
-    send_all(
-        "seg", OWNERS, lambda peer: out_ref.at[peer], got_ref, send_sems.at[0], recv_sems.at[0]
-    )
-    got_ref[me] = out_ref[me]
-    loads[8].wait()
-    lay_out_bricks(bricks_ref, wide_ref, brick_ref)
-    wait_all(got_ref, OWNERS, recv_sems.at[0])
-
-    unpack(got_ref, half_ref, place_ref, basis_ref)
-    extra = place_ref[3]
-    send_all(
-        "grp", GROUPS, lambda peer: place_ref, places_ref, send_sems.at[1], recv_sems.at[1]
-    )
-    own_places = pltpu.make_async_copy(place_ref, places_ref.at[group], own_sems.at[0])
-    own_places.start()
-    wait_all(ids_ref, OWNERS, recv_sems.at[7])
-    ids = pltpu.make_async_copy(ids_ref, id_smem, own_sems.at[2])
-    ids.start()
-    ids.wait()
-    interpolate(brick_ref, place_ref, basis_ref, id_smem, raw_ref)
-    sums_ref[:, 0, :] = segment_sums(raw_ref, extra)
-
-    send_all(
-        "seg", OWNERS, lambda peer: sums_ref.at[peer // 2], back_ref,
-        send_sems.at[2], recv_sems.at[2],
-    )
-    back_ref[me] = sums_ref[me // 2]
-    send_all("grp", GROUPS, lambda peer: raw_ref, raws_ref, send_sems.at[3], recv_sems.at[3])
-    own_raws = pltpu.make_async_copy(raw_ref, raws_ref.at[group], own_sems.at[1])
-    own_raws.start()
-    wait_all(back_ref, OWNERS, recv_sems.at[2])
-    choice = choice_ref[...]
-    ray_ref[...] = to_rays(back_ref[:, 0, :], choice)[0:4]
-
-    send_all("seg", OWNERS, lambda peer: ray_ref, rays_ref, send_sems.at[4], recv_sems.at[4])
-    rays_ref[me] = ray_ref[...]
-    wait_all(rays_ref, OWNERS, recv_sems.at[4])
-    colour, grads = composite(
-        [rays_ref[:, v, :] for v in range(3)], rays_ref[:, 3, :], target_ref[...]
-    )
-    for v in range(3):
-        colour_ref[v : v + 1, :] = colour[v]
-    slot_out_ref[:, 0, :] = to_slots(grads, choice)
-
-    send_all(
-        "seg", OWNERS, lambda peer: slot_out_ref.at[peer], slots_ref,
-        send_sems.at[5], recv_sems.at[5],
-    )
-    slots_ref[me] = slot_out_ref[me]
-    wait_all(slots_ref, OWNERS, recv_sems.at[5])
-    pick = jnp.where((iota((8, OWNERS), 1) // 2) % 8 == iota((8, OWNERS), 0), 1.0, 0.0)
-    grads_ref[...] = exact_dot(pick, slots_ref[:, 0, :])
-    send_all(
-        "grp", GROUPS, lambda peer: grads_ref, all_grads_ref, send_sems.at[6], recv_sems.at[6]
-    )
-    all_grads_ref[group] = grads_ref[...]
-    wait_all(all_grads_ref, GROUPS, recv_sems.at[6])
-    own_places.wait()
-    own_raws.wait()
-    wait_all(places_ref, GROUPS, recv_sems.at[1])
-    wait_all(raws_ref, GROUPS, recv_sems.at[3])
-    wait_all(got_ref, OWNERS, send_sems.at[0])
-    wait_all(ids_ref, OWNERS, send_sems.at[7])
-    wait_all(places_ref, GROUPS, send_sems.at[1])
-    wait_all(back_ref, OWNERS, send_sems.at[2])
-    wait_all(raws_ref, GROUPS, send_sems.at[3])
-    wait_all(rays_ref, OWNERS, send_sems.at[4])
-    wait_all(slots_ref, OWNERS, send_sems.at[5])
-    wait_all(all_grads_ref, GROUPS, send_sems.at[6])
-
-
-def render(*operands):
-    return pl.pallas_call(
-        render_kernel,
-        out_shape=(
-            jax.ShapeDtypeStruct((3, RAYS), F32),
-            jax.ShapeDtypeStruct((GROUPS, 4, CHUNKS, 128), F32),
-            jax.ShapeDtypeStruct((GROUPS, 4, CHUNKS, 128), F32),
-            jax.ShapeDtypeStruct((GROUPS, 8, 128), F32),
-        ),
-        in_specs=[ANY] * 9,
-        out_specs=(VMEM, ANY, ANY, VMEM),
-        scratch_shapes=[pltpu.VMEM(x.shape, x.dtype) for x in operands]
-        + [
-            pltpu.VMEM((OWNERS, SLOTS * RAYS), F32),
-            pltpu.VMEM((OWNERS, 2, 128), F32),
-            pltpu.VMEM((OWNERS, 2, 128), F32),
-            pltpu.VMEM((4, BRICKS * 32, 128), F32),
-            pltpu.VMEM((BRICKS, 32, VOXELS), BF16),
-            pltpu.VMEM((OWNERS, 128), F32),
-            pltpu.VMEM((OWNERS, 1, 128), I32),
-            pltpu.VMEM((OWNERS, 1, 128), I32),
-            pltpu.SMEM((OWNERS, 1, 128), I32),
-            pltpu.VMEM((4, CHUNKS, 128), F32),
-            pltpu.VMEM((4, CHUNKS, 128), F32),
-            pltpu.VMEM((CHUNKS * 8, 128), F32),
-            pltpu.VMEM((CHUNKS, 1, 128), F32),
-            pltpu.VMEM((OWNERS, 1, 128), F32),
-            pltpu.VMEM((4, RAYS), F32),
-            pltpu.VMEM((OWNERS, 4, RAYS), F32),
-            pltpu.VMEM((OWNERS, 1, 128), F32),
-            pltpu.VMEM((OWNERS, 1, 128), F32),
-            pltpu.VMEM((8, 128), F32),
-            pltpu.SemaphoreType.DMA((9,)),
-            pltpu.SemaphoreType.DMA((8,)),
-            pltpu.SemaphoreType.DMA((8,)),
-            pltpu.SemaphoreType.DMA((3,)),
-        ],
-        compiler_params=pltpu.CompilerParams(
-            collective_id=0, has_side_effects=True, vmem_limit_bytes=64 << 20
-        ),
-        name="render",
-    )(*operands)
 
 
 def plan_chunks(extra):
@@ -527,58 +351,292 @@
     return jnp.concatenate([tile, turn, last], axis=0).astype(I32)
 
 
-def gradient_kernel(
-    places_hbm, raws_hbm, grads_hbm, colour_hbm, out_ref, colour_ref,
-    places_ref, raws_ref, grads_ref, tiles_ref, table_vmem, table_smem, slot_ref, total_ref, sems,
-):
-    load_places = pltpu.make_async_copy(places_hbm, places_ref, sems.at[0])
-    load_raws = pltpu.make_async_copy(raws_hbm, raws_ref, sems.at[2])
-    load_places.start()
-    load_raws.start()
-    load_grads = pltpu.make_async_copy(grads_hbm, grads_ref, sems.at[3])
-    load_grads.start()
-    load_colour = pltpu.make_async_copy(colour_hbm, colour_ref, sems.at[4])
-    load_colour.start()
-    tiles_ref[pl.ds(ALL_CHUNKS * 8, 8), :] = jnp.zeros((8, 128), F32)
-    total_ref[...] = jnp.zeros_like(total_ref)
-    load_places.wait()
-    extra = jnp.concatenate([places_ref[g, 3] for g in range(GROUPS)], axis=0)
-    table_vmem[...] = plan_chunks(extra)
-    plan = pltpu.make_async_copy(table_vmem, table_smem, sems.at[1])
-    plan.start()
-    for g in range(GROUPS):
-        for q in range(4):
-            tiles_ref[pl.ds(g * CHUNKS * 8 + 4 + q, CHUNKS, stride=8), :] = places_ref[g, q]
-
-    load_grads.wait()
-    load_colour.wait()
+def shade_all(raws_ref, extra):
+    raw = [
+        jnp.concatenate([raws_ref[g, v] for g in range(GROUPS)], axis=0) for v in range(4)
+    ]
+    _, through, opaque, (step, remains) = march(raw[0], extra)
+    light = through * opaque
+    radiance = [sigmoid(value) for value in raw[1:]]
+    return radiance + [light, through * remains, step * sigmoid(raw[0])]
+
+
+def sample_gradients(grads_ref, shades_ref, slot_ref, tiles_ref):
     row, lane = iota((128, 128), 0), iota((128, 128), 1)
+    grads = jnp.concatenate([grads_ref[g] for g in range(GROUPS)], axis=0)
     for part in range(4):
         for v in range(4):
             spread = jnp.where(row == part * 32 + (lane // 16) * 4 + v, 1.0, 0.0)
-            wide = exact_dot(grads_ref[...], spread)
+            wide = exact_dot(grads, spread)
             for g in range(GROUPS):
                 slot_ref[v, pl.ds(g * CHUNKS + part * 8, 8), :] = wide[g * 8 : g * 8 + 8]
-    load_raws.wait()
-
-    def raw(v):
-        return jnp.concatenate([raws_ref[g, v] for g in range(GROUPS)], axis=0)
-
-    density = raw(0)
-    optical, through, opaque, (step, remains) = march(density, extra)
-    light = through * opaque
+    light = shades_ref[3]
     mixed = jnp.zeros((ALL_CHUNKS, 128), F32)
     for v in range(3):
-        radiance = sigmoid(raw(1 + v))
+        radiance = shades_ref[v]
         grad_colour = slot_ref[v]
         mixed += grad_colour * radiance
         tiles_ref[pl.ds(1 + v, ALL_CHUNKS, stride=8), :] = (
             grad_colour * light * radiance * (1.0 - radiance)
         )
     later = jnp.where((row // 16 == lane // 16) & (row > lane), 1.0, 0.0)
-    grad_optical = through * remains * mixed - exact_dot(light * mixed, later) + slot_ref[3]
-    tiles_ref[pl.ds(0, ALL_CHUNKS, stride=8), :] = grad_optical * step * sigmoid(density)
-    plan.wait()
+    grad_optical = shades_ref[4] * mixed - exact_dot(light * mixed, later) + slot_ref[3]
+    tiles_ref[pl.ds(0, ALL_CHUNKS, stride=8), :] = grad_optical * shades_ref[5]
+
+
+def to_rays(sums, choice):
+    half = lax.rem(lax.axis_index("seg"), 2)
+    turned = pltpu.roll(sums, lax.rem(128 - half * 32, 128), 1)
+    found = exact_dot(jnp.transpose(turned)[0:32], choice)
+    total = jnp.zeros((8, RAYS), F32)
+    for j in range(SLOTS):
+        total += found[8 * j : 8 * j + 8, RAYS * j : RAYS * j + RAYS]
+    return total
+
+
+def composite(colours, taus, target):
+    me = lax.axis_index("seg")
+    lower = jnp.where(iota((OWNERS, OWNERS), 1) < iota((OWNERS, OWNERS), 0), 1.0, 0.0)
+    through = jnp.exp(-exact_dot(lower, taus))
+    depth = iota((OWNERS, RAYS), 0)
+    here = jnp.sum(jnp.where(depth == me, through, 0.0), axis=0, keepdims=True)
+    colour, grad_colour = [], []
+    grad_tau = jnp.zeros((1, RAYS), F32)
+    for v in range(3):
+        contrib = through * colours[v]
+        colour.append(jnp.sum(contrib, axis=0, keepdims=True))
+        behind = jnp.sum(jnp.where(depth > me, contrib, 0.0), axis=0, keepdims=True)
+        misfit = LOSS_SCALE * (colour[v] - target[v : v + 1])
+        grad_colour.append(here * misfit)
+        grad_tau -= misfit * behind
+    return colour, grad_colour + [grad_tau]
+
+
+def to_slots(grads, choice):
+    me = lax.axis_index("seg")
+    row = iota((SLOTS * 4, RAYS), 0)
+    block = jnp.zeros((SLOTS * 4, RAYS), F32)
+    for v in range(4):
+        block = jnp.where(row % 4 == v, grads[v], block)
+    wide = jnp.concatenate(
+        [jnp.where(row // 4 == j, block, 0.0) for j in range(SLOTS)], axis=1
+    )
+    wide = jnp.concatenate([wide, jnp.zeros((112, SLOTS * RAYS), F32)], axis=0)
+    placed = exact_dot(choice, wide, NT)
+    return pltpu.roll(placed, (me // 16) * 32 + lax.rem(me, 2) * 16, 1)
+
+
+def render_kernel(
+    owner_hbm, slot_hbm, wanted_hbm, cells_hbm, fracs_hbm, angles_hbm, step_hbm, target_hbm,
+    bricks_hbm,
+    colour_ref, tiles_ref, table_ref,
+    owner_ref, slot_ref, wanted_ref, cells_ref, fracs_ref, angles_ref, step_ref, target_ref,
+    bricks_ref,
+    choice_ref, out_ref, got_ref, wide_ref, brick_ref, half_ref, numbers_ref, ids_ref, id_vmem, id_smem,
+    place_ref, raw_ref, basis_ref,
+    sums_ref, back_ref, ray_ref, rays_ref, slot_out_ref, slots_ref, grads_ref,
+    places_ref, raws_ref, all_grads_ref, shades_ref, slot_grads_ref,
+    load_sems, send_sems, recv_sems, ring_sends, ring_recvs, own_sem,
+):
+    loads = [
+        pltpu.make_async_copy(source, target, load_sems.at[k])
+        for k, (source, target) in enumerate(
+            [
+                (owner_hbm, owner_ref), (slot_hbm, slot_ref), (wanted_hbm, wanted_ref),
+                (cells_hbm, cells_ref), (fracs_hbm, fracs_ref), (angles_hbm, angles_ref),
+                (step_hbm, step_ref), (target_hbm, target_ref), (bricks_hbm, bricks_ref),
+            ]
+        )
+    ]
+    for load in loads:
+        load.start()
+    met = greet([("seg", OWNERS), ("grp", GROUPS)])
+    for load in loads[:8]:
+        load.wait()
+    me = lax.axis_index("seg")
+    group = lax.axis_index("grp")
+
+    def pass_places(step):
+        ring_start(places_ref, step, ring_sends.at[0], ring_recvs.at[0])
+
+    def take_places(step):
+        ring_wait(places_ref, step, ring_recvs.at[0], True)
+
+    def pass_raws(step):
+        ring_start(raws_ref, step, ring_sends.at[1], ring_recvs.at[1])
+
+    def take_raws(step):
+        ring_wait(raws_ref, step, ring_recvs.at[1], True)
+
+    choice, numbers, first, second = pack(
+        owner_ref[...], slot_ref[...], wanted_ref[...], cells_ref[...], fracs_ref[...],
+        ray_basis(angles_ref[...]), step_ref[...],
+    )
+    choice_ref[...] = choice
+    out_ref[:, 0, :] = first
+    out_ref[:, 1, :] = second
+    numbers_ref[:, 0, :] = numbers
+    met()
+    send_all(
+        "seg", OWNERS, lambda peer: numbers_ref.at[peer], ids_ref, send_sems.at[7], recv_sems.at[7]
+    )
+    ids_ref[me] = numbers_ref[me]
+    send_all(
+        "seg", OWNERS, lambda peer: out_ref.at[peer], got_ref, send_sems.at[0], recv_sems.at[0]
+    )
+    got_ref[me] = out_ref[me]
+    loads[8].wait()
+    lay_out_bricks(bricks_ref, wide_ref, brick_ref)
+    wait_all(got_ref, OWNERS, recv_sems.at[0])
+
+    unpack(got_ref, half_ref, place_ref, basis_ref)
+    extra = place_ref[3]
+    places_ref[group] = place_ref[...]
+    pass_places(1)
+    wait_all(ids_ref, OWNERS, recv_sems.at[7])
+    for half in range(2):
+        id_vmem[half : half + 1, :] = jnp.sum(
+            ids_ref[32 * half : 32 * half + 32, 0, :], axis=0, keepdims=True
+        )
+    ids = pltpu.make_async_copy(id_vmem, id_smem, own_sem)
+    ids.start()
+    ids.wait()
+    interpolate(brick_ref, place_ref, basis_ref, id_smem, raw_ref)
+    take_places(1)
+    pass_places(2)
+    raws_ref[group] = raw_ref[...]
+    pass_raws(1)
+    sums_ref[:, 0, :] = segment_sums(raw_ref, extra)
+
+    send_all(
+        "seg", OWNERS, lambda peer: sums_ref.at[peer // 2], back_ref,
+        send_sems.at[2], recv_sems.at[2],
+    )
+    back_ref[me] = sums_ref[me // 2]
+    take_places(2)
+    pass_places(3)
+    take_raws(1)
+    pass_raws(2)
+    wait_all(back_ref, OWNERS, recv_sems.at[2])
+    choice = choice_ref[...]
+    ray_ref[...] = to_rays(back_ref[:, 0, :], choice)[0:4]
+
+    send_all("seg", OWNERS, lambda peer: ray_ref, rays_ref, send_sems.at[4], recv_sems.at[4])
+    rays_ref[me] = ray_ref[...]
+    take_places(3)
+    pass_places(4)
+    take_raws(2)
+    pass_raws(3)
+    take_places(4)
+    all_extra = jnp.concatenate([places_ref[g, 3] for g in range(GROUPS)], axis=0)
+    table_ref[...] = plan_chunks(all_extra)
+    wait_all(rays_ref, OWNERS, recv_sems.at[4])
+    colour, grads = composite(
+        [rays_ref[:, v, :] for v in range(3)], rays_ref[:, 3, :], target_ref[...]
+    )
+    for v in range(3):
+        colour_ref[v : v + 1, :] = colour[v]
+    slot_out_ref[:, 0, :] = to_slots(grads, choice)
+
+    send_all(
+        "seg", OWNERS, lambda peer: slot_out_ref.at[peer], slots_ref,
+        send_sems.at[5], recv_sems.at[5],
+    )
+    slots_ref[me] = slot_out_ref[me]
+    take_raws(3)
+    pass_raws(4)
+    for g in range(GROUPS):
+        for q in range(4):
+            tiles_ref[pl.ds(g * CHUNKS * 8 + 4 + q, CHUNKS, stride=8), :] = places_ref[g, q]
+    wait_all(slots_ref, OWNERS, recv_sems.at[5])
+    pick = jnp.where((iota((8, OWNERS), 1) // 2) % 8 == iota((8, OWNERS), 0), 1.0, 0.0)
+    grads_ref[...] = exact_dot(pick, slots_ref[:, 0, :])
+    send_all(
+        "grp", GROUPS, lambda peer: grads_ref, all_grads_ref, send_sems.at[6], recv_sems.at[6]
+    )
+    all_grads_ref[group] = grads_ref[...]
+    take_raws(4)
+    for k, value in enumerate(shade_all(raws_ref, all_extra)):
+        shades_ref[k] = value
+    wait_all(all_grads_ref, GROUPS, recv_sems.at[6])
+    sample_gradients(all_grads_ref, shades_ref, slot_grads_ref, tiles_ref)
+    wait_all(got_ref, OWNERS, send_sems.at[0])
+    wait_all(ids_ref, OWNERS, send_sems.at[7])
+    wait_all(back_ref, OWNERS, send_sems.at[2])
+    for step in range(1, 5):
+        ring_wait(places_ref, step, ring_sends.at[0], False)
+        ring_wait(raws_ref, step, ring_sends.at[1], False)
+    wait_all(rays_ref, OWNERS, send_sems.at[4])
+    wait_all(slots_ref, OWNERS, send_sems.at[5])
+    wait_all(all_grads_ref, GROUPS, send_sems.at[6])
+
+
+def render(*operands):
+    return pl.pallas_call(
+        render_kernel,
+        out_shape=(
+            jax.ShapeDtypeStruct((3, RAYS), F32),
+            jax.ShapeDtypeStruct((ALL_CHUNKS * 8, 128), F32),
+            jax.ShapeDtypeStruct((24, TABLE), I32),
+        ),
+        in_specs=[ANY] * 9,
+        out_specs=(VMEM, VMEM, VMEM),
+        scratch_shapes=[pltpu.VMEM(x.shape, x.dtype) for x in operands]
+        + [
+            pltpu.VMEM((OWNERS, SLOTS * RAYS), F32),
+            pltpu.VMEM((OWNERS, 2, 128), F32),
+            pltpu.VMEM((OWNERS, 2, 128), F32),
+            pltpu.VMEM((4, BRICKS * 32, 128), F32),
+            pltpu.VMEM((BRICKS, 32, VOXELS), BF16),
+            pltpu.VMEM((OWNERS, 128), F32),
+            pltpu.VMEM((OWNERS, 1, 128), I32),
+            pltpu.VMEM((OWNERS, 1, 128), I32),
+            pltpu.VMEM((2, 128), I32),
+            pltpu.SMEM((2, 128), I32),
+            pltpu.VMEM((4, CHUNKS, 128), F32),
+            pltpu.VMEM((4, CHUNKS, 128), F32),
+            pltpu.VMEM((CHUNKS * 8, 128), F32),
+            pltpu.VMEM((CHUNKS, 1, 128), F32),
+            pltpu.VMEM((OWNERS, 1, 128), F32),
+            pltpu.VMEM((4, RAYS), F32),
+            pltpu.VMEM((OWNERS, 4, RAYS), F32),
+            pltpu.VMEM((OWNERS, 1, 128), F32),
+            pltpu.VMEM((OWNERS, 1, 128), F32),
+            pltpu.VMEM((8, 128), F32),
+            pltpu.VMEM((GROUPS, 4, CHUNKS, 128), F32),
+            pltpu.VMEM((GROUPS, 4, CHUNKS, 128), F32),
+            pltpu.VMEM((GROUPS, 8, 128), F32),
+            pltpu.VMEM((6, ALL_CHUNKS, 128), F32),
+            pltpu.VMEM((4, ALL_CHUNKS, 128), F32),
+            pltpu.SemaphoreType.DMA((9,)),
+            pltpu.SemaphoreType.DMA((8,)),
+            pltpu.SemaphoreType.DMA((8,)),
+            pltpu.SemaphoreType.DMA((2, 2, 4)),
+            pltpu.SemaphoreType.DMA((2, 2, 4)),
+            pltpu.SemaphoreType.DMA,
+        ],
+        compiler_params=pltpu.CompilerParams(
+            collective_id=0, has_side_effects=True, vmem_limit_bytes=64 << 20
+        ),
+        name="render",
+    )(*operands)
+
+
+def gradient_kernel(
+    tiles_hbm, table_hbm, colour_hbm, out_hbm, colour_ref,
+    tiles_ref, table_smem, total_ref, out_ref, sems, out_sems,
+):
+    loads = [
+        pltpu.make_async_copy(table_hbm, table_smem, sems.at[0]),
+        pltpu.make_async_copy(tiles_hbm, tiles_ref.at[pl.ds(0, ALL_CHUNKS * 8)], sems.at[1]),
+        pltpu.make_async_copy(colour_hbm, colour_ref, sems.at[2]),
+    ]
+    for load in loads:
+        load.start()
+    tiles_ref[pl.ds(ALL_CHUNKS * 8, 8), :] = jnp.zeros((8, 128), F32)
+    total_ref[...] = jnp.zeros_like(total_ref)
+    for load in loads:
+        load.wait()
 
     lane_group = iota((8, 128), 1) // 16
     pick = lane_group * 16 + iota((8, 128), 0) + 1
@@ -626,49 +684,51 @@
         parts = [one(turn * UNROLL + k) for k in range(UNROLL)]
         for k in range(UNROLL):
             b = table_smem[16, turn * UNROLL + k]
-            rows = pl.ds(pl.multiple_of(b * 128, 128), 128)
+            rows = pl.ds(pl.multiple_of(b * BRICK_ROWS, 8), 128)
             total_ref[rows, :] += parts[k]
         return carry
 
     lax.fori_loop(0, (table_smem[17, 0] + UNROLL - 1) // UNROLL, several, 0)
 
+    outs = []
     for c in range(COEF):
         for x in range(4):
             out_ref[c, :, x * 128 : x * 128 + 128] = total_ref[
-                pl.ds(x * 32 + ROW_OF[c], BRICKS, stride=128), :
+                pl.ds(x * 32 + ROW_OF[c], BRICKS, stride=BRICK_ROWS), :
             ]
-
-
-def gradient(places, raws, grads, colour):
+        outs.append(pltpu.make_async_copy(out_ref.at[c], out_hbm.at[c], out_sems.at[c]))
+        outs[c].start()
+    for out in outs:
+        out.wait()
+
+
+def gradient(tiles, table, colour):
     return pl.pallas_call(
         gradient_kernel,
         out_shape=(
             jax.ShapeDtypeStruct((COEF, BRICKS, VOXELS), F32),
             jax.ShapeDtypeStruct((3, RAYS), F32),
         ),
-        in_specs=[ANY] * 4,
-        out_specs=(VMEM, VMEM),
+        in_specs=[ANY] * 3,
+        out_specs=(ANY, VMEM),
         scratch_shapes=[
-            pltpu.VMEM((GROUPS, 4, CHUNKS, 128), F32),
-            pltpu.VMEM((GROUPS, 4, CHUNKS, 128), F32),
-            pltpu.VMEM((GROUPS * 8, 128), F32),
             pltpu.VMEM((ALL_CHUNKS * 8 + 8, 128), F32),
-            pltpu.VMEM((24, TABLE), I32),
             pltpu.SMEM((24, TABLE), I32),
-            pltpu.VMEM((4, ALL_CHUNKS, 128), F32),
-            pltpu.VMEM((BRICKS * 128, 128), F32),
-            pltpu.SemaphoreType.DMA((5,)),
+            pltpu.VMEM((BRICKS * BRICK_ROWS, 128), F32),
+            pltpu.VMEM((COEF, BRICKS, VOXELS), F32),
+            pltpu.SemaphoreType.DMA((3,)),
+            pltpu.SemaphoreType.DMA((COEF,)),
         ],
         compiler_params=pltpu.CompilerParams(vmem_limit_bytes=64 << 20),
         name="gradient",
-    )(places, raws, grads, colour)
+    )(tiles, table, colour)
 
 
 def local(
     bricks, requests, seg_owner, seg_slot, sample_cells, sample_fracs,
     ray_angles, ray_step, pixel_target,
 ):
-    colour, places, raws, grads = render(
+    colour, tiles, table = render(
         seg_owner.reshape(1, RAYS),
         seg_slot.reshape(1, RAYS),
         jnp.transpose(requests.reshape(OWNERS, 2)),
@@ -679,7 +739,7 @@
         pixel_target,
         bricks,
     )
-    return gradient(places, raws, grads.reshape(GROUPS * 8, 128), colour)
+    return gradient(tiles, table, colour)
 
 
 def solution(mesh):

time: 81.6 us -> 75.5 us (0.925)
  the two profiles are of different devices: /device:TPU:20 before, /device:TPU:48 now
where the time goes in v3:
time: 75.5 us; the launch traced here: 75.3 us
  Pallas kernels  74.7 us (99%)
    pallas_call x1, Pallas kernels, render(): pl.pallas_call(render_kernel, out_shape=(jax.ShapeDtypeStruct((3, RAYS),...  52.7 us
    pallas_call x1, Pallas kernels, gradient(): pl.pallas_call(gradient_kernel, out_shape=(jax.ShapeDtypeStruct((COEF, BR...  21.9 us

profile of v3, /device:TPU:48, one launch (start us, length us, event | category | flops | bytes accessed | tf_op | source)
XLA Modules:
  0.0 75.3 jit_solution(83492774404581853)
XLA Ops:
  0.6 52.7 %render.1 = (f32[3,128]{1,0:T(4,128)}, f32[2048,128]{1,0:T(8,128)}, s32[24,384]{1,0:T(8,128)}) custom-call(s32[1,128]{1,0:T(1,128)} %bitcast.10, s32[1,128]{1,0:T(1,128)} %slot_hbm.1, s32[2,64]{1,0:T(2,128)} %bitcast.9, s32[16,128]{1,0:T(8,128)} %bitcast.8, f32[48,128]{1,0:T(8,128)} %bitcast.7, f32[2,128]{1,0:T(2,128)} %angles_hbm.1, f32[1,128]{1,0:T(1,128)} %bitcast.11, ...), custom_call_target="tpu_custom_call" | custom-call | tf_op jit(solution)/shard_map/render/pallas_call | solution.py:575
  53.4 21.9 %gradient.1 = (f32[28,48,512]{2,1,0:T(8,128)}, f32[3,128]{1,0:T(4,128)}) custom-call(f32[2048,128]{1,0:T(8,128)} %get-tuple-element.5.tiles_hbm, s32[24,384]{1,0:T(8,128)} %get-tuple-element.6.table_hbm, f32[3,128]{1,0:T(4,128)} %get-tuple-element.7.colour_hbm), custom_call_target="tpu_custom_call" | custom-call | tf_op jit(solution)/shard_map/gradient/pallas_call | solution.py:706

commit v4 on v3

--- a/solution.py
+++ b/solution.py
@@ -101,6 +101,7 @@
     chosen = [mine & (rank == j) for j in range(SLOTS)]
     choice = jnp.concatenate([jnp.where(one, 1.0, 0.0) for one in chosen], axis=1)
     lane = iota((OWNERS, RAYS), 1) - lax.rem(lax.axis_index("seg"), 32) * SLOTS
+    spots = owner * SLOTS + rank
     bricks = jnp.zeros((OWNERS, RAYS), I32)
     for j in range(SLOTS):
         named = jnp.sum(jnp.where(chosen[j], brick, 0), axis=1, keepdims=True)
@@ -128,7 +129,7 @@
         return jnp.concatenate(parts, axis=1)
 
     return (
-        choice,
+        spots,
         bricks,
         exact_dot(choice, placed(place_x, place_y), NT),
         exact_dot(choice, placed(place_z, extra), NT),
@@ -203,16 +204,16 @@
 def lay_out_bricks(bricks_ref, wide_ref, brick_ref):
     for c in range(COEF, 32):
         for x in range(4):
-            wide_ref[x, pl.ds(c, BRICKS, stride=32), :] = jnp.zeros((BRICKS, 128), F32)
+            wide_ref[x, pl.ds(c, BRICKS, stride=40), :] = jnp.zeros((BRICKS, 128), F32)
     for c in range(COEF):
         for x in range(4):
-            wide_ref[x, pl.ds(ROW_OF[c], BRICKS, stride=32), :] = bricks_ref[
+            wide_ref[x, pl.ds(ROW_OF[c], BRICKS, stride=40), :] = bricks_ref[
                 c, :, x * 128 : x * 128 + 128
             ].astype(F32)
 
     def narrow(turn, carry):
         for k in range(8):
-            rows = pl.ds(pl.multiple_of(turn * 256 + k * 32, 32), 32)
+            rows = pl.ds(pl.multiple_of(turn * 320 + k * 40, 8), 32)
             for x in range(4):
                 brick_ref[turn * 8 + k, :, x * 128 : x * 128 + 128] = wide_ref[
                     x, rows, :
@@ -280,8 +281,8 @@
     row, lane = iota((128, 128), 0), iota((128, 128), 1)
     for v in range(4):
         part = optical if v == 3 else light * sigmoid(raw_ref[1 + v])
-        total += exact_dot(part, jnp.where(lane == (row // 16) * 8 + v, 1.0, 0.0))
-    return total
+        total += exact_dot(part, jnp.where(lane == (row // 16) * 4 + v, 1.0, 0.0))
+    return sum(pltpu.roll(total[8 * k : 8 * k + 8], 32 * k, 1) if k else total[0:8] for k in range(4))
 
 
 def march(density, extra):
@@ -384,46 +385,55 @@
     tiles_ref[pl.ds(0, ALL_CHUNKS, stride=8), :] = grad_optical * shades_ref[5]
 
 
-def to_rays(sums, choice):
-    half = lax.rem(lax.axis_index("seg"), 2)
-    turned = pltpu.roll(sums, lax.rem(128 - half * 32, 128), 1)
-    found = exact_dot(jnp.transpose(turned)[0:32], choice)
-    total = jnp.zeros((8, RAYS), F32)
-    for j in range(SLOTS):
-        total += found[8 * j : 8 * j + 8, RAYS * j : RAYS * j + RAYS]
-    return total
+def to_rays(sums_ref, spots_ref, rays_ref):
+    owner = iota((OWNERS, RAYS), 0)
+    slot = iota((16, RAYS), 0) // 4
+    for row in range(8):
+        across = jnp.transpose(sums_ref[:, row, :])
+        high, rest = split(across)
+        middle, low = split(across - high.astype(F32))
+        for part in range(4):
+            for half in range(2):
+                s = 2 * (part * 8 + row) + half
+                rows = slice(part * 32 + half * 16, part * 32 + half * 16 + 16)
+                spots = spots_ref[s, 1:2, :]
+                hits = jnp.where(spots // SLOTS == owner, 1.0, 0.0).astype(BF16)
+                three = fast_dot(
+                    jnp.concatenate([high[rows], middle[rows], low[rows]], axis=0), hits
+                )
+                found = three[0:16] + three[16:32] + three[32:48]
+                found = jnp.where(spots % SLOTS == slot, found, 0.0)
+                found = found[0:8] + found[8:16]
+                rays_ref[s] = found[0:4] + found[4:8]
 
 
 def composite(colours, taus, target):
-    me = lax.axis_index("seg")
-    lower = jnp.where(iota((OWNERS, OWNERS), 1) < iota((OWNERS, OWNERS), 0), 1.0, 0.0)
-    through = jnp.exp(-exact_dot(lower, taus))
-    depth = iota((OWNERS, RAYS), 0)
-    here = jnp.sum(jnp.where(depth == me, through, 0.0), axis=0, keepdims=True)
-    colour, grad_colour = [], []
-    grad_tau = jnp.zeros((1, RAYS), F32)
+    depth, other = iota((OWNERS, OWNERS), 0), iota((OWNERS, OWNERS), 1)
+    through = jnp.exp(-exact_dot(jnp.where(other < depth, 1.0, 0.0), taus))
+    behind = jnp.where(other > depth, 1.0, 0.0)
+    colour, grads = [], []
+    grad_tau = jnp.zeros((OWNERS, RAYS), F32)
     for v in range(3):
         contrib = through * colours[v]
         colour.append(jnp.sum(contrib, axis=0, keepdims=True))
-        behind = jnp.sum(jnp.where(depth > me, contrib, 0.0), axis=0, keepdims=True)
         misfit = LOSS_SCALE * (colour[v] - target[v : v + 1])
-        grad_colour.append(here * misfit)
-        grad_tau -= misfit * behind
-    return colour, grad_colour + [grad_tau]
-
-
-def to_slots(grads, choice):
+        grads.append(through * misfit)
+        grad_tau -= misfit * exact_dot(behind, contrib)
+    return colour, grads + [grad_tau]
+
+
+def to_slots(grads, spots):
     me = lax.axis_index("seg")
-    row = iota((SLOTS * 4, RAYS), 0)
-    block = jnp.zeros((SLOTS * 4, RAYS), F32)
-    for v in range(4):
-        block = jnp.where(row % 4 == v, grads[v], block)
-    wide = jnp.concatenate(
-        [jnp.where(row // 4 == j, block, 0.0) for j in range(SLOTS)], axis=1
-    )
-    wide = jnp.concatenate([wide, jnp.zeros((112, SLOTS * RAYS), F32)], axis=0)
-    placed = exact_dot(choice, wide, NT)
-    return pltpu.roll(placed, (me // 16) * 32 + lax.rem(me, 2) * 16, 1)
+    depth = iota((OWNERS, 128), 0)
+    place = iota((OWNERS, 128), 1) - (depth // 16) * 32 - (depth % 2) * 16
+    placed = jnp.zeros((OWNERS, 128), F32)
+    for j in range(SLOTS):
+        here = spots == me * SLOTS + j
+        for v in range(4):
+            value = jnp.sum(jnp.where(here, grads[v], 0.0), axis=1, keepdims=True)
+            placed = jnp.where(place == j * 4 + v, value, placed)
+    pick = jnp.where((iota((8, OWNERS), 1) // 2) % 8 == iota((8, OWNERS), 0), 1.0, 0.0)
+    return exact_dot(pick, placed)
 
 
 def render_kernel(
@@ -432,9 +442,9 @@
     colour_ref, tiles_ref, table_ref,
     owner_ref, slot_ref, wanted_ref, cells_ref, fracs_ref, angles_ref, step_ref, target_ref,
     bricks_ref,
-    choice_ref, out_ref, got_ref, wide_ref, brick_ref, half_ref, numbers_ref, ids_ref, id_vmem, id_smem,
+    out_ref, got_ref, wide_ref, brick_ref, half_ref, numbers_ref, ids_ref, id_vmem, id_smem,
     place_ref, raw_ref, basis_ref,
-    sums_ref, back_ref, ray_ref, rays_ref, slot_out_ref, slots_ref, grads_ref,
+    sums_ref, all_sums_ref, rays_ref, grads_ref,
     places_ref, raws_ref, all_grads_ref, shades_ref, slot_grads_ref,
     load_sems, send_sems, recv_sems, ring_sends, ring_recvs, own_sem,
 ):
@@ -468,14 +478,14 @@
     def take_raws(step):
         ring_wait(raws_ref, step, ring_recvs.at[1], True)
 
-    choice, numbers, first, second = pack(
+    spots, numbers, first, second = pack(
         owner_ref[...], slot_ref[...], wanted_ref[...], cells_ref[...], fracs_ref[...],
         ray_basis(angles_ref[...]), step_ref[...],
     )
-    choice_ref[...] = choice
     out_ref[:, 0, :] = first
     out_ref[:, 1, :] = second
     numbers_ref[:, 0, :] = numbers
+    numbers_ref[:, 1, :] = jnp.broadcast_to(spots, (OWNERS, RAYS))
     met()
     send_all(
         "seg", OWNERS, lambda peer: numbers_ref.at[peer], ids_ref, send_sems.at[7], recv_sems.at[7]
@@ -506,55 +516,41 @@
     pass_places(2)
     raws_ref[group] = raw_ref[...]
     pass_raws(1)
-    sums_ref[:, 0, :] = segment_sums(raw_ref, extra)
+    sums_ref[...] = segment_sums(raw_ref, extra)
 
     send_all(
-        "seg", OWNERS, lambda peer: sums_ref.at[peer // 2], back_ref,
-        send_sems.at[2], recv_sems.at[2],
-    )
-    back_ref[me] = sums_ref[me // 2]
+        "seg", OWNERS, lambda peer: sums_ref, all_sums_ref, send_sems.at[2], recv_sems.at[2]
+    )
+    all_sums_ref[me] = sums_ref[...]
     take_places(2)
     pass_places(3)
     take_raws(1)
     pass_raws(2)
-    wait_all(back_ref, OWNERS, recv_sems.at[2])
-    choice = choice_ref[...]
-    ray_ref[...] = to_rays(back_ref[:, 0, :], choice)[0:4]
-
-    send_all("seg", OWNERS, lambda peer: ray_ref, rays_ref, send_sems.at[4], recv_sems.at[4])
-    rays_ref[me] = ray_ref[...]
     take_places(3)
     pass_places(4)
     take_raws(2)
     pass_raws(3)
+    wait_all(all_sums_ref, OWNERS, recv_sems.at[2])
+    to_rays(all_sums_ref, ids_ref, rays_ref)
+    take_raws(3)
+    pass_raws(4)
+    colour, grads = composite(
+        [rays_ref[:, v, :] for v in range(3)], rays_ref[:, 3, :], target_ref[...]
+    )
+    for v in range(3):
+        colour_ref[v : v + 1, :] = colour[v]
+    grads_ref[...] = to_slots(grads, ids_ref[:, 1, :])
+
+    send_all(
+        "grp", GROUPS, lambda peer: grads_ref, all_grads_ref, send_sems.at[6], recv_sems.at[6]
+    )
+    all_grads_ref[group] = grads_ref[...]
     take_places(4)
     all_extra = jnp.concatenate([places_ref[g, 3] for g in range(GROUPS)], axis=0)
     table_ref[...] = plan_chunks(all_extra)
-    wait_all(rays_ref, OWNERS, recv_sems.at[4])
-    colour, grads = composite(
-        [rays_ref[:, v, :] for v in range(3)], rays_ref[:, 3, :], target_ref[...]
-    )
-    for v in range(3):
-        colour_ref[v : v + 1, :] = colour[v]
-    slot_out_ref[:, 0, :] = to_slots(grads, choice)
-
-    send_all(
-        "seg", OWNERS, lambda peer: slot_out_ref.at[peer], slots_ref,
-        send_sems.at[5], recv_sems.at[5],
-    )
-    slots_ref[me] = slot_out_ref[me]
-    take_raws(3)
-    pass_raws(4)
     for g in range(GROUPS):
         for q in range(4):
             tiles_ref[pl.ds(g * CHUNKS * 8 + 4 + q, CHUNKS, stride=8), :] = places_ref[g, q]
-    wait_all(slots_ref, OWNERS, recv_sems.at[5])
-    pick = jnp.where((iota((8, OWNERS), 1) // 2) % 8 == iota((8, OWNERS), 0), 1.0, 0.0)
-    grads_ref[...] = exact_dot(pick, slots_ref[:, 0, :])
-    send_all(
-        "grp", GROUPS, lambda peer: grads_ref, all_grads_ref, send_sems.at[6], recv_sems.at[6]
-    )
-    all_grads_ref[group] = grads_ref[...]
     take_raws(4)
     for k, value in enumerate(shade_all(raws_ref, all_extra)):
         shades_ref[k] = value
@@ -562,12 +558,10 @@
     sample_gradients(all_grads_ref, shades_ref, slot_grads_ref, tiles_ref)
     wait_all(got_ref, OWNERS, send_sems.at[0])
     wait_all(ids_ref, OWNERS, send_sems.at[7])
-    wait_all(back_ref, OWNERS, send_sems.at[2])
+    wait_all(all_sums_ref, OWNERS, send_sems.at[2])
     for step in range(1, 5):
         ring_wait(places_ref, step, ring_sends.at[0], False)
         ring_wait(raws_ref, step, ring_sends.at[1], False)
-    wait_all(rays_ref, OWNERS, send_sems.at[4])
-    wait_all(slots_ref, OWNERS, send_sems.at[5])
     wait_all(all_grads_ref, GROUPS, send_sems.at[6])
 
 
@@ -583,25 +577,21 @@
         out_specs=(VMEM, VMEM, VMEM),
         scratch_shapes=[pltpu.VMEM(x.shape, x.dtype) for x in operands]
         + [
-            pltpu.VMEM((OWNERS, SLOTS * RAYS), F32),
             pltpu.VMEM((OWNERS, 2, 128), F32),
             pltpu.VMEM((OWNERS, 2, 128), F32),
-            pltpu.VMEM((4, BRICKS * 32, 128), F32),
+            pltpu.VMEM((4, BRICKS * 40, 128), F32),
             pltpu.VMEM((BRICKS, 32, VOXELS), BF16),
             pltpu.VMEM((OWNERS, 128), F32),
-            pltpu.VMEM((OWNERS, 1, 128), I32),
-            pltpu.VMEM((OWNERS, 1, 128), I32),
+            pltpu.VMEM((OWNERS, 2, 128), I32),
+            pltpu.VMEM((OWNERS, 2, 128), I32),
             pltpu.VMEM((2, 128), I32),
             pltpu.SMEM((2, 128), I32),
             pltpu.VMEM((4, CHUNKS, 128), F32),
             pltpu.VMEM((4, CHUNKS, 128), F32),
             pltpu.VMEM((CHUNKS * 8, 128), F32),
-            pltpu.VMEM((CHUNKS, 1, 128), F32),
-            pltpu.VMEM((OWNERS, 1, 128), F32),
-            pltpu.VMEM((4, RAYS), F32),
+            pltpu.VMEM((8, 128), F32),
+            pltpu.VMEM((OWNERS, 8, 128), F32),
             pltpu.VMEM((OWNERS, 4, RAYS), F32),
-            pltpu.VMEM((OWNERS, 1, 128), F32),
-            pltpu.VMEM((OWNERS, 1, 128), F32),
             pltpu.VMEM((8, 128), F32),
             pltpu.VMEM((GROUPS, 4, CHUNKS, 128), F32),
             pltpu.VMEM((GROUPS, 4, CHUNKS, 128), F32),
@@ -674,11 +664,12 @@
             )
 
         high, low = both(high), both(low)
-        return fast_dot(
-            jnp.concatenate([left_high, left_high, left_low], axis=1),
-            jnp.concatenate([high, low, high], axis=1),
+        four = fast_dot(
+            jnp.concatenate([left_high, left_low], axis=0),
+            jnp.concatenate([high, low], axis=0),
             NT,
         )
+        return four[0:128, 0:128] + four[0:128, 128:256] + four[128:256, 0:128]
 
     def several(turn, carry):
         parts = [one(turn * UNROLL + k) for k in range(UNROLL)]

time: 75.5 us -> 64.5 us (0.85)
  the two profiles are of different devices: /device:TPU:48 before, /device:TPU:20 now
where the time goes in v4:
time: 64.5 us; the launch traced here: 64.4 us
  Pallas kernels  63.7 us (99%)
    pallas_call x1, Pallas kernels, render(): pl.pallas_call(render_kernel, out_shape=(jax.ShapeDtypeStruct((3, RAYS),...  45.3 us
    pallas_call x1, Pallas kernels, gradient(): pl.pallas_call(gradient_kernel, out_shape=(jax.ShapeDtypeStruct((COEF, BR...  18.4 us

profile of v4, /device:TPU:20, one launch (start us, length us, event | category | flops | bytes accessed | tf_op | source)
XLA Modules:
  0.0 64.4 jit_solution(15844181624491722667)
XLA Ops:
  0.6 45.3 %render.1 = (f32[3,128]{1,0:T(4,128)}, f32[2048,128]{1,0:T(8,128)}, s32[24,384]{1,0:T(8,128)}) custom-call(s32[1,128]{1,0:T(1,128)} %bitcast.10, s32[1,128]{1,0:T(1,128)} %slot_hbm.1, s32[2,64]{1,0:T(2,128)} %bitcast.9, s32[16,128]{1,0:T(8,128)} %bitcast.8, f32[48,128]{1,0:T(8,128)} %bitcast.7, f32[2,128]{1,0:T(2,128)} %angles_hbm.1, f32[1,128]{1,0:T(1,128)} %bitcast.11, ...), custom_call_target="tpu_custom_call" | custom-call | tf_op jit(solution)/shard_map/render/pallas_call | solution.py:569
  45.9 18.4 %gradient.1 = (f32[28,48,512]{2,1,0:T(8,128)}, f32[3,128]{1,0:T(4,128)}) custom-call(f32[2048,128]{1,0:T(8,128)} %get-tuple-element.5.tiles_hbm, s32[24,384]{1,0:T(8,128)} %get-tuple-element.6.table_hbm, f32[3,128]{1,0:T(4,128)} %get-tuple-element.7.colour_hbm), custom_call_target="tpu_custom_call" | custom-call | tf_op jit(solution)/shard_map/gradient/pallas_call | solution.py:697

commit v5 on v4

--- a/solution.py
+++ b/solution.py
@@ -11,6 +11,7 @@
 VOXELS = 512
 SAMP = 16
 OWNERS = 64
+CHIPS = OWNERS // 2
 GROUPS = 8
 SLOTS = 4
 BRICKS = 48
@@ -129,8 +130,7 @@
         return jnp.concatenate(parts, axis=1)
 
     return (
-        spots,
-        bricks,
+        bricks * 256 + spots,
         exact_dot(choice, placed(place_x, place_y), NT),
         exact_dot(choice, placed(place_z, extra), NT),
     )
@@ -238,7 +238,7 @@
         basis_ref[pl.ds(k, CHUNKS, stride=8), :] = basis[:, k * 128 : k * 128 + 128]
 
 
-def interpolate(brick_ref, place_ref, basis_ref, id_smem, raw_ref):
+def interpolate(brick_ref, place_ref, basis_ref, id_smem, raw_ref, half):
     lane_group = iota((32, 128), 1) // 16
 
     def one(chunk):
@@ -271,7 +271,8 @@
             one(turn * FUNROLL + k)
         return carry
 
-    lax.fori_loop(0, CHUNKS // FUNROLL, several, 0)
+    turns = CHUNKS // FUNROLL // 2
+    lax.fori_loop(half * turns, (half + 1) * turns, several, 0)
 
 
 def segment_sums(raw_ref, extra):
@@ -386,17 +387,18 @@
 
 
 def to_rays(sums_ref, spots_ref, rays_ref):
-    owner = iota((OWNERS, RAYS), 0)
+    spot = iota((OWNERS, RAYS), 0)
+    owner = lax.rem(spot, CHIPS) * 2 + spot // CHIPS
     slot = iota((16, RAYS), 0) // 4
     for row in range(8):
-        across = jnp.transpose(sums_ref[:, row, :])
+        across = jnp.transpose(sums_ref[:, :, row, :].reshape(OWNERS, 128))
         high, rest = split(across)
         middle, low = split(across - high.astype(F32))
         for part in range(4):
             for half in range(2):
                 s = 2 * (part * 8 + row) + half
                 rows = slice(part * 32 + half * 16, part * 32 + half * 16 + 16)
-                spots = spots_ref[s, 1:2, :]
+                spots = spots_ref[s]
                 hits = jnp.where(spots // SLOTS == owner, 1.0, 0.0).astype(BF16)
                 three = fast_dot(
                     jnp.concatenate([high[rows], middle[rows], low[rows]], axis=0), hits
@@ -442,7 +444,7 @@
     colour_ref, tiles_ref, table_ref,
     owner_ref, slot_ref, wanted_ref, cells_ref, fracs_ref, angles_ref, step_ref, target_ref,
     bricks_ref,
-    out_ref, got_ref, wide_ref, brick_ref, half_ref, numbers_ref, ids_ref, id_vmem, id_smem,
+    out_ref, got_ref, wide_ref, brick_ref, half_ref, numbers_ref, ids_ref, spots_ref, id_vmem, id_smem,
     place_ref, raw_ref, basis_ref,
     sums_ref, all_sums_ref, rays_ref, grads_ref,
     places_ref, raws_ref, all_grads_ref, shades_ref, slot_grads_ref,
@@ -478,14 +480,13 @@
     def take_raws(step):
         ring_wait(raws_ref, step, ring_recvs.at[1], True)
 
-    spots, numbers, first, second = pack(
+    numbers, first, second = pack(
         owner_ref[...], slot_ref[...], wanted_ref[...], cells_ref[...], fracs_ref[...],
         ray_basis(angles_ref[...]), step_ref[...],
     )
     out_ref[:, 0, :] = first
     out_ref[:, 1, :] = second
     numbers_ref[:, 0, :] = numbers
-    numbers_ref[:, 1, :] = jnp.broadcast_to(spots, (OWNERS, RAYS))
     met()
     send_all(
         "seg", OWNERS, lambda peer: numbers_ref.at[peer], ids_ref, send_sems.at[7], recv_sems.at[7]
@@ -506,32 +507,59 @@
     wait_all(ids_ref, OWNERS, recv_sems.at[7])
     for half in range(2):
         id_vmem[half : half + 1, :] = jnp.sum(
-            ids_ref[32 * half : 32 * half + 32, 0, :], axis=0, keepdims=True
+            ids_ref[32 * half : 32 * half + 32, 0, :] // 256, axis=0, keepdims=True
         )
     ids = pltpu.make_async_copy(id_vmem, id_smem, own_sem)
     ids.start()
+    spots_ref[:, 0, :] = lax.rem(ids_ref[:, 0, :], 256)
     ids.wait()
-    interpolate(brick_ref, place_ref, basis_ref, id_smem, raw_ref)
+    interpolate(brick_ref, place_ref, basis_ref, id_smem, raw_ref, 0)
     take_places(1)
     pass_places(2)
+    interpolate(brick_ref, place_ref, basis_ref, id_smem, raw_ref, 1)
+    take_places(2)
+    pass_places(3)
     raws_ref[group] = raw_ref[...]
     pass_raws(1)
     sums_ref[...] = segment_sums(raw_ref, extra)
 
-    send_all(
-        "seg", OWNERS, lambda peer: sums_ref, all_sums_ref, send_sems.at[2], recv_sems.at[2]
-    )
-    all_sums_ref[me] = sums_ref[...]
-    take_places(2)
-    pass_places(3)
+    chip, core = me // 2, lax.rem(me, 2)
+
+    def to_chip(turn, carry):
+        pltpu.make_async_remote_copy(
+            src_ref=sums_ref,
+            dst_ref=all_sums_ref.at[core, chip],
+            send_sem=send_sems.at[2],
+            recv_sem=recv_sems.at[2],
+            device_id={"seg": lax.rem(chip + turn, CHIPS) * 2 + core},
+            device_id_type=MESH,
+        ).start()
+        return carry
+
+    lax.fori_loop(1, CHIPS, to_chip, 0, unroll=31)
+    all_sums_ref[core, chip] = sums_ref[...]
+    take_places(3)
+    pass_places(4)
     take_raws(1)
     pass_raws(2)
-    take_places(3)
-    pass_places(4)
+    wait_all(all_sums_ref.at[core], CHIPS, recv_sems.at[2])
+    across = pltpu.make_async_remote_copy(
+        src_ref=all_sums_ref.at[core],
+        dst_ref=all_sums_ref.at[core],
+        send_sem=send_sems.at[4],
+        recv_sem=recv_sems.at[4],
+        device_id={"seg": me + 1 - 2 * core},
+        device_id_type=MESH,
+    )
+    across.start()
     take_raws(2)
     pass_raws(3)
-    wait_all(all_sums_ref, OWNERS, recv_sems.at[2])
-    to_rays(all_sums_ref, ids_ref, rays_ref)
+    take_places(4)
+    all_extra = jnp.concatenate([places_ref[g, 3] for g in range(GROUPS)], axis=0)
+    table_ref[...] = plan_chunks(all_extra)
+    other = all_sums_ref.at[1 - core]
+    pltpu.make_async_copy(other, other, recv_sems.at[4]).wait()
+    to_rays(all_sums_ref, spots_ref, rays_ref)
     take_raws(3)
     pass_raws(4)
     colour, grads = composite(
@@ -539,15 +567,12 @@
     )
     for v in range(3):
         colour_ref[v : v + 1, :] = colour[v]
-    grads_ref[...] = to_slots(grads, ids_ref[:, 1, :])
+    grads_ref[...] = to_slots(grads, spots_ref[:, 0, :])
 
     send_all(
         "grp", GROUPS, lambda peer: grads_ref, all_grads_ref, send_sems.at[6], recv_sems.at[6]
     )
     all_grads_ref[group] = grads_ref[...]
-    take_places(4)
-    all_extra = jnp.concatenate([places_ref[g, 3] for g in range(GROUPS)], axis=0)
-    table_ref[...] = plan_chunks(all_extra)
     for g in range(GROUPS):
         for q in range(4):
             tiles_ref[pl.ds(g * CHUNKS * 8 + 4 + q, CHUNKS, stride=8), :] = places_ref[g, q]
@@ -558,7 +583,8 @@
     sample_gradients(all_grads_ref, shades_ref, slot_grads_ref, tiles_ref)
     wait_all(got_ref, OWNERS, send_sems.at[0])
     wait_all(ids_ref, OWNERS, send_sems.at[7])
-    wait_all(all_sums_ref, OWNERS, send_sems.at[2])
+    wait_all(all_sums_ref.at[core], CHIPS, send_sems.at[2])
+    across.wait_send()
     for step in range(1, 5):
         ring_wait(places_ref, step, ring_sends.at[0], False)
         ring_wait(raws_ref, step, ring_sends.at[1], False)
@@ -582,15 +608,16 @@
             pltpu.VMEM((4, BRICKS * 40, 128), F32),
             pltpu.VMEM((BRICKS, 32, VOXELS), BF16),
             pltpu.VMEM((OWNERS, 128), F32),
-            pltpu.VMEM((OWNERS, 2, 128), I32),
-            pltpu.VMEM((OWNERS, 2, 128), I32),
+            pltpu.VMEM((OWNERS, 1, 128), I32),
+            pltpu.VMEM((OWNERS, 1, 128), I32),
+            pltpu.VMEM((OWNERS, 1, 128), I32),
             pltpu.VMEM((2, 128), I32),
             pltpu.SMEM((2, 128), I32),
             pltpu.VMEM((4, CHUNKS, 128), F32),
             pltpu.VMEM((4, CHUNKS, 128), F32),
             pltpu.VMEM((CHUNKS * 8, 128), F32),
             pltpu.VMEM((8, 128), F32),
-            pltpu.VMEM((OWNERS, 8, 128), F32),
+            pltpu.VMEM((2, CHIPS, 8, 128), F32),
             pltpu.VMEM((OWNERS, 4, RAYS), F32),
             pltpu.VMEM((8, 128), F32),
             pltpu.VMEM((GROUPS, 4, CHUNKS, 128), F32),

time: 64.5 us -> 69.4 us (1.076)
  the two profiles are of different devices: /device:TPU:20 before, /device:TPU:18 now
where the time goes in v5:
time: 69.4 us; the launch traced here: 69.2 us
  Pallas kernels  68.6 us (99%)
    pallas_call x1, Pallas kernels, render(): pl.pallas_call(render_kernel, out_shape=(jax.ShapeDtypeStruct((3, RAYS),...  50.1 us
    pallas_call x1, Pallas kernels, gradient(): pl.pallas_call(gradient_kernel, out_shape=(jax.ShapeDtypeStruct((COEF, BR...  18.4 us

profile of v5, /device:TPU:18, one launch (start us, length us, event | category | flops | bytes accessed | tf_op | source)
XLA Modules:
  0.0 69.2 jit_solution(4761459064201310807)
XLA Ops:
  0.6 50.1 %render.1 = (f32[3,128]{1,0:T(4,128)}, f32[2048,128]{1,0:T(8,128)}, s32[24,384]{1,0:T(8,128)}) custom-call(s32[1,128]{1,0:T(1,128)} %bitcast.10, s32[1,128]{1,0:T(1,128)} %slot_hbm.1, s32[2,64]{1,0:T(2,128)} %bitcast.9, s32[16,128]{1,0:T(8,128)} %bitcast.8, f32[48,128]{1,0:T(8,128)} %bitcast.7, f32[2,128]{1,0:T(2,128)} %angles_hbm.1, f32[1,128]{1,0:T(1,128)} %bitcast.11, ...), custom_call_target="tpu_custom_call" | custom-call | tf_op jit(solution)/shard_map/render/pallas_call | solution.py:595
  50.8 18.4 %gradient.1 = (f32[28,48,512]{2,1,0:T(8,128)}, f32[3,128]{1,0:T(4,128)}) custom-call(f32[2048,128]{1,0:T(8,128)} %get-tuple-element.5.tiles_hbm, s32[24,384]{1,0:T(8,128)} %get-tuple-element.6.table_hbm, f32[3,128]{1,0:T(4,128)} %get-tuple-element.7.colour_hbm), custom_call_target="tpu_custom_call" | custom-call | tf_op jit(solution)/shard_map/gradient/pallas_call | solution.py:724
